TPU v7x, 128 devices: a whole 4x4x4 slice. The times are simulated.
128 devices in a mesh: section: 4 (over z_hi, core), expert: 32 (over z_lo, x, y).
Axes of the slice: x: 4, y: 4, z: 4 (z_hi: 2, z_lo: 2; z = z_hi * 2 + z_lo), core: 2. Of those that a mesh axis runs over, the one named last changes fastest.
Arguments:
- activations: bfloat16 [4, 4096, 3584], P('section', 'expert'), may hold values from -21 to 21
- norm_gain: float32 [4, 3584], P('section'), may hold values from 0.1 to 1.9
- w_gate: bfloat16 [4, 32, 3584, 1024], P('section', 'expert'), may hold values from -0.09375 to 0.09375
- w_up: bfloat16 [4, 32, 3584, 1024], P('section', 'expert'), may hold values from -0.09375 to 0.09375
- w_down: bfloat16 [4, 32, 1024, 3584], P('section', 'expert'), may hold values from -0.1875 to 0.1875
- routes: int32 [2, 4, 4096, 2], P(None, 'section', 'expert'), may hold values from 0 to 31, all different within a row; in each aligned block of 128 rows (0 to 127, 128 to 255, ..., all dimensions but the last counted through in order) at most 16 rows name the same one
- gate_logits: float32 [2, 4, 4096, 2], P(None, 'section', 'expert'), may hold values from -6 to 6
Outputs:
- advanced: bfloat16 [4, 4096, 3584], P('section', 'expert')
Inputs may be any that keep to these rules, and one draw needn't show every extreme that they name: `routes`: within each aligned block of 128 token rows (the rows of one device for one step and section) each row names 2 different experts and no expert is named by more than 16 rows; some expert is named by exactly 16 rows.
All inputs are finite; a program needn't handle non-finite values.
Results may differ from a plain program's by a relative error of at most 0.0057.
Values may be sent and summed in bfloat16 or wider, within the bound.
No kernel may reach another device: no remote copies, remote signals or barrier semaphores. Data moves between devices by JAX's collectives and lax.ppermute only.
A program may use at most 192 MiB of HBM per device.

v0:
```python
import jax
import jax.numpy as jnp
from jax import lax
from jax.sharding import PartitionSpec as P

TOP = 2
STEPS = 2


EPSILON = 1e-06


def shifted(value, axis, steps):
    count = lax.axis_size(axis)
    pairs = [(source, (source + steps) % count) for source in range(count)]
    return lax.ppermute(value, axis, pairs)


def normalize(values_in, gain):
    values = values_in.astype(jnp.float32)
    scaling = lax.rsqrt(jnp.mean(values * values, axis=-1, keepdims=True) + EPSILON)
    return (values * scaling * gain).astype(jnp.bfloat16)


def gate_share(logits):
    lifted = jax.nn.sigmoid(logits)
    return lifted / jnp.sum(lifted, axis=-1, keepdims=True)


def slot_table(chosen, number_experts, capacity):
    token_count, choices = chosen.shape
    flattened = chosen.reshape(-1)
    indicator = (flattened[:, None] == jnp.arange(number_experts, dtype=jnp.int32)[None, :]).astype(
        jnp.int32
    )
    earlier = jnp.cumsum(indicator, axis=0) - indicator
    position = jnp.sum(earlier * indicator, axis=1)
    places = jnp.arange(capacity, dtype=jnp.int32)
    matches = (indicator.T[:, None, :] == 1) & (position[None, None, :] == places[None, :, None])
    owners = jnp.arange(token_count * choices, dtype=jnp.int32) // choices
    picked = jnp.sum(jnp.where(matches, owners[None, None, :] + 1, 0), axis=2) - 1
    picked = jnp.where(picked < 0, token_count, picked)
    return (position.reshape(token_count, choices), picked)


def expert_forward(rows, gate_matrix, up_matrix, down_matrix):
    gate = jnp.dot(rows, gate_matrix, preferred_element_type=jnp.float32)
    upward = jnp.dot(rows, up_matrix, preferred_element_type=jnp.float32)
    hidden = (jax.nn.silu(gate) * upward).astype(jnp.bfloat16)
    return jnp.dot(hidden, down_matrix, preferred_element_type=jnp.float32).astype(jnp.bfloat16)


def give_back(produced):
    return lax.all_to_all(produced, "expert", split_axis=0, concat_axis=0, tiled=True)


def on_device(activations, norm_gain, w_gate, w_up, w_down, routes, gate_logits):
    groups = lax.axis_size("expert")
    token_count = activations.shape[1]
    width = activations.shape[2]
    capacity = 2 * token_count * TOP // groups
    gate_matrix = w_gate[0, 0]
    up_matrix = w_up[0, 0]
    down_matrix = w_down[0, 0]
    gain = norm_gain[0]
    current = activations[0]
    for step_index in range(STEPS):
        chosen = routes[step_index, 0]
        shares = gate_share(gate_logits[step_index, 0])
        normed = normalize(current, gain)
        slots, picks = slot_table(chosen, groups, capacity)
        wanted = lax.all_to_all(picks, "expert", split_axis=0, concat_axis=0, tiled=True)
        piece = lax.all_gather(normed[None], "expert", axis=0, tiled=True)
        extended = jnp.concatenate(
            [piece, jnp.zeros((piece.shape[0], 1, width), jnp.bfloat16)], axis=1
        )
        collected = jax.vmap(lambda rows, index: rows[index])(extended, wanted)
        senders = collected.shape[0]
        count = collected.shape[1]
        produced = expert_forward(
            collected.reshape(senders * count, width), gate_matrix, up_matrix, down_matrix
        )
        returned = give_back(produced.reshape(senders, count, width))
        fetched = returned[chosen, slots]
        mixed = jnp.sum(shares[..., None] * fetched.astype(jnp.float32), axis=1)
        current = (current.astype(jnp.float32) + mixed).astype(jnp.bfloat16)
        current = shifted(current, "section", 1)
    return current[None]


def solution(mesh):
    in_specs = (
        P("section", "expert", None),
        P("section", None),
        P("section", "expert", None, None),
        P("section", "expert", None, None),
        P("section", "expert", None, None),
        P(None, "section", "expert", None),
        P(None, "section", "expert", None),
    )
    out_specs = P("section", "expert", None)
    return jax.shard_map(
        on_device, mesh=mesh, in_specs=in_specs, out_specs=out_specs, check_vma=False
    )
```

profile of v0, /device:TPU:0, one launch (start us, length us, event | category | flops | bytes accessed | tf_op | source)
XLA Modules:
  0.0 1029.9 jit_solution(4818431937189372210)
XLA Ops:
  15.6 17.0 %all_to_all.28 = s32[32,1,16]{2,1,0:T(1,128)S(1)} all-to-all(s32[32,1,16]{2,1,0:T(1,128)S(1)} %bitcast.131), channel_id=1, replica_groups=mesh['section'=4,'expert'=32] {'expert'}, dimensions={0} | all-to-all | bytes 4096 | tf_op jit(solution)/shard_map/all_to_all | solution.py:72
  32.9 302.3 %all-gather.4.cloned.1.call-done = bf16[32,128,3584]{2,1,0:T(8,128)(2,1)} async-done(((bf16[1,128,3584]{2,1,0:T(8,128)(2,1)}), bf16[32,128,3584]{2,1,0:T(8,128)(2,1)}) %all-gather.4.cloned.1.call-update) | async-done | bytes 29360144 | tf_op jit(solution)/shard_map/all_gather | solution.py:73
  335.2 27.7 %copy.46 = bf16[32,128,3584]{2,0,1:T(8,128)(2,1)} copy(bf16[32,128,3584]{2,1,0:T(8,128)(2,1)} %all-gather.4.cloned.1.call-done) | data formatting | bytes 58720256 | tf_op jit(solution)/shard_map/all_gather | solution.py:73
  362.9 20.3 %concatenate.12 = bf16[32,129,3584]{2,0,1:T(8,128)(2,1)} pad(bf16[32,128,3584]{2,0,1:T(8,128)(2,1)} %copy.46, bf16[]{:T(256)} %constant.47.clone.1), padding=0_0x0_1x0_0 | pad | bytes 58949632 | tf_op jit(solution)/shard_map/concatenate | solution.py:74
  383.2 20.6 %gather_fusion.2 = bf16[512,3584]{1,0:T(8,128)(2,1)} fusion(bf16[32,129,3584]{2,0,1:T(8,128)(2,1)} %concatenate.12, s32[512]{0:T(512)S(1)} %reshape.471), kind=kCustom, calls=%fused_computation.2 | custom fusion | bytes 7344128 | tf_op jit(solution)/shard_map/vmap()/gather | solution.py:77
  403.8 9.5 fusion.6
  413.3 16.6 %fusion.12 = bf16[512,3584]{1,0:T(8,128)(2,1)} fusion(bf16[1,1,1024,3584]{3,2,1,0:T(8,128)(2,1)} %param.11, f32[512,1024]{1,0:T(8,128)} %fusion.6, bf16[512,3584]{1,0:T(8,128)(2,1)} %gather_fusion.2, bf16[1,1,3584,1024]{3,2,1,0:T(8,128)(2,1)} %param.9), kind=kOutput, calls=%fused_computation.16 | convolution fusion | flops 7521173504 | bytes 24117248 | tf_op jit(solution)/shard_map/dot_general | solution.py:50
  429.8 5.0 all-to-all-start.1
  435.7 50.9 %all-to-all-done.1 = bf16[32,16,3584]{2,1,0:T(8,128)(2,1)} async-done(((bf16[32,16,3584]{2,1,0:T(8,128)(2,1)}), bf16[32,16,3584]{2,1,0:T(8,128)(2,1)}, u32[]{:S(2)}, u32[]{:S(2)}) %all-to-all-start.1) | async-done | bytes 3670048 | tf_op jit(solution)/shard_map/all_to_all | solution.py:54
  486.6 5.5 gather_fusion
  495.6 7.4 multiply_reduce_fusion.1
  503.3 14.3 %collective-permute-done = bf16[128,3584]{1,0:T(8,128)(2,1)S(1)} collective-permute-done((bf16[128,3584]{1,0:T(8,128)(2,1)S(1)}, bf16[128,3584]{1,0:T(8,128)(2,1)S(1)}, u32[]{:S(2)}, u32[]{:S(2)}) %collective-permute-start) | collective-permute-done | bytes 917536 | tf_op jit(solution)/shard_map/ppermute | solution.py:16
  519.1 15.7 %all_to_all.29 = s32[32,1,16]{2,1,0:T(1,128)S(1)} all-to-all(s32[32,1,16]{2,1,0:T(1,128)S(1)} %bitcast.132), channel_id=1, replica_groups=mesh['section'=4,'expert'=32] {'expert'}, dimensions={0} | all-to-all | bytes 4096 | tf_op jit(solution)/shard_map/all_to_all | solution.py:72
  535.0 306.4 %all-gather.6.cloned.1.call-done = bf16[4096,3584]{1,0:T(8,128)(2,1)} async-done(((bf16[128,3584]{1,0:T(8,128)(2,1)}), bf16[4096,3584]{1,0:T(8,128)(2,1)}) %all-gather.6.cloned.1.call-update) | async-done | bytes 29360144 | tf_op jit(solution)/shard_map/all_gather | solution.py:73
  841.4 27.7 %copy.53 = bf16[32,128,3584]{2,0,1:T(8,128)(2,1)} copy(bf16[32,128,3584]{2,1,0:T(8,128)(2,1)} %bitcast.127) | data formatting | bytes 58720256 | tf_op jit(solution)/shard_map/all_gather | solution.py:73
  869.2 20.3 %concatenate.14 = bf16[32,129,3584]{2,0,1:T(8,128)(2,1)} pad(bf16[32,128,3584]{2,0,1:T(8,128)(2,1)} %copy.53, bf16[]{:T(256)} %constant.47.clone.1), padding=0_0x0_1x0_0 | pad | bytes 58949632 | tf_op jit(solution)/shard_map/concatenate | solution.py:74
  889.4 21.0 %gather_fusion.3 = bf16[512,3584]{1,0:T(8,128)(2,1)} fusion(bf16[32,129,3584]{2,0,1:T(8,128)(2,1)} %concatenate.14, s32[512]{0:T(512)S(1)} %reshape.477), kind=kCustom, calls=%fused_computation.3 | custom fusion | bytes 7344128 | tf_op jit(solution)/shard_map/vmap()/gather | solution.py:77
  910.5 9.5 fusion.4
  920.0 16.6 %fusion.15 = bf16[512,3584]{1,0:T(8,128)(2,1)} fusion(bf16[1,1,1024,3584]{3,2,1,0:T(8,128)(2,1)} %param.11, f32[512,1024]{1,0:T(8,128)} %fusion.4, bf16[512,3584]{1,0:T(8,128)(2,1)} %gather_fusion.3, bf16[1,1,3584,1024]{3,2,1,0:T(8,128)(2,1)} %param.9), kind=kOutput, calls=%fused_computation.17 | convolution fusion | flops 7521173504 | bytes 24117248 | tf_op jit(solution)/shard_map/dot_general | solution.py:50
  936.5 5.2 all-to-all-start.3
  942.1 48.5 %all-to-all-done.3 = bf16[32,16,3584]{2,1,0:T(8,128)(2,1)} async-done(((bf16[32,16,3584]{2,1,0:T(8,128)(2,1)}), bf16[32,16,3584]{2,1,0:T(8,128)(2,1)}, u32[]{:S(2)}, u32[]{:S(2)}) %all-to-all-start.3) | async-done | bytes 3670048 | tf_op jit(solution)/shard_map/all_to_all | solution.py:54
  990.6 5.5 gather_fusion.1
  999.7 7.3 multiply_reduce_fusion
  1007.3 14.6 %collective-permute-done.1 = bf16[128,3584]{1,0:T(8,128)(2,1)S(1)} collective-permute-done((bf16[128,3584]{1,0:T(8,128)(2,1)S(1)}, bf16[128,3584]{1,0:T(8,128)(2,1)S(1)}, u32[]{:S(2)}, u32[]{:S(2)}) %collective-permute-start.1) | collective-permute-done | bytes 917536 | tf_op jit(solution)/shard_map/ppermute | solution.py:16
  (75 shorter events, 20.7 us)
Async XLA Ops:
  6.5 4.6 copy-start.6
  6.5 328.7 %all-gather.4.cloned.1.call-start = ((), (), s32[]{:S(2)}) async-start(), calls=%async_computation.4 | async-start | bytes 30277632 | tf_op jit(solution)/shard_map/all_gather | solution.py:73
  11.7 21.0 %copy-start.1 = (s32[1,1,128,2]{3,2,1,0:T(8,128)}, s32[1,1,128,2]{3,2,1,0:T(8,128)S(1)}, u32[]{:S(2)}) copy-start(s32[1,1,128,2]{3,2,1,0:T(8,128)S(1)} %copy.60) | copy-start | bytes 3076
  13.9 0.6 copy-start.3
  429.8 5.7 copy-start.5
  429.8 56.8 %all-to-all-start.1 = ((bf16[32,16,3584]{2,1,0:T(8,128)(2,1)}), bf16[32,16,3584]{2,1,0:T(8,128)(2,1)}, u32[]{:S(2)}, u32[]{:S(2)}) async-start(bf16[32,16,3584]{2,1,0:T(8,128)(2,1)} %bitcast.128), calls=%async_computation.1 | async-start | bytes 7340032 | tf_op jit(solution)/shard_map/all_to_all | solution.py:54
  434.8 406.7 %all-gather.6.cloned.1.call-start = ((), (), s32[]{:S(2)}) async-start(), calls=%async_computation.5 | async-start | bytes 30277632 | tf_op jit(solution)/shard_map/all_gather | solution.py:73
  495.6 7.4 copy-start
  503.2 14.4 %collective-permute-start = (bf16[128,3584]{1,0:T(8,128)(2,1)S(1)}, bf16[128,3584]{1,0:T(8,128)(2,1)S(1)}, u32[]{:S(2)}, u32[]{:S(2)}) collective-permute-start(bf16[128,3584]{1,0:T(8,128)(2,1)S(1)} %fusion.21), channel_id=1, source_target_pairs={{0,32},{32,64},{64,96},{96,0},{1,33},{33,65},{65,97},{97,1},{2,34}... | collective-permute-start | bytes 2752520 | tf_op jit(solution)/shard_map/ppermute | solution.py:16
  936.5 5.2 copy-start.4
  936.5 5.4 copy-start.2
  936.5 54.1 %all-to-all-start.3 = ((bf16[32,16,3584]{2,1,0:T(8,128)(2,1)}), bf16[32,16,3584]{2,1,0:T(8,128)(2,1)}, u32[]{:S(2)}, u32[]{:S(2)}) async-start(bf16[32,16,3584]{2,1,0:T(8,128)(2,1)} %bitcast.129), calls=%async_computation.3 | async-start | bytes 7340032 | tf_op jit(solution)/shard_map/all_to_all | solution.py:54
  1007.2 14.7 %collective-permute-start.1 = (bf16[128,3584]{1,0:T(8,128)(2,1)S(1)}, bf16[128,3584]{1,0:T(8,128)(2,1)S(1)}, u32[]{:S(2)}, u32[]{:S(2)}) collective-permute-start(bf16[128,3584]{1,0:T(8,128)(2,1)S(1)} %fusion.27), channel_id=1, source_target_pairs={{0,32},{32,64},{64,96},{96,0},{1,33},{33,65},{65,97},{97,1},{2,34}... | collective-permute-start | bytes 2752520 | tf_op jit(solution)/shard_map/ppermute | solution.py:16
Sparse Core Ops, SparseCore 0:
  11.3 323.8 all-gather.3
  519.2 322.1 all-gather.5
where the time goes:
time: 1040 us; the launch traced here: 1030 us
  waiting for transfers between devices  737 us (71%)
  local copies, waits for them, and re-layouts  159 us (15%)
  matrix products  52.1 us (5%)
  blocking collectives  32.7 us (3%)
  other arithmetic  23.9 us (2%)
  between operations  13.9 us (1%)
  starting transfers between devices  10.7 us (1%)
    all_gather x2, waiting for transfers between devices, on_device(): piece = lax.all_gather(normed[None], 'expert', axis=0, tiled=True)  609 us
    all_to_all x2, waiting for transfers between devices, give_back(): lax.all_to_all(produced, 'expert', split_axis=0, concat_axis=0, tiled=True)  99.4 us
    all_gather x2, local copies, waits for them, and re-layouts, on_device(): piece = lax.all_gather(normed[None], 'expert', axis=0, tiled=True)  55.4 us
    gather x6, local copies, waits for them, and re-layouts, on_device(): collected = jax.vmap(lambda rows, index: rows[index])(extended, wanted)  42 us
    concatenate x2, local copies, waits for them, and re-layouts, on_device(): jnp.concatenate([piece, jnp.zeros((piece.shape[0], 1, width), jnp.bfloat1...  40.5 us
    dot_general x2, matrix products, expert_forward(): jnp.dot(hidden, down_matrix, preferred_element_type=jnp.float32)  33.1 us
    all_to_all x2, blocking collectives, on_device(): lax.all_to_all(picks, 'expert', split_axis=0, concat_axis=0, tiled=True)  32.7 us
    ppermute x2, waiting for transfers between devices, shifted(): return lax.ppermute(value, axis, pairs)  28.9 us
  transfers between devices with their start and end apart: 6, of which 6 were waited for; matrix products, arithmetic and copies ran while one was open for 1% of the time, Pallas kernels for 0%

commit v1 on v0

v1 whole, which is shorter than its diff:
```python
import functools

import jax
import jax.numpy as jnp
from jax import lax
from jax.experimental import pallas as pl
from jax.experimental.pallas import tpu as pltpu
from jax.sharding import PartitionSpec as P

TOP = 2
STEPS = 2
EPSILON = 1e-06
VMEM_LIMIT = 56 * 1024 * 1024


def slot_keys(routes, experts, capacity):
    rows = routes.shape[0]
    lanes = lax.broadcasted_iota(jnp.int32, (rows, experts), 1)
    named = [(routes[:, k : k + 1] == lanes).astype(jnp.float32) for k in range(TOP)]
    counts = sum(named).astype(jnp.bfloat16)
    below = lax.broadcasted_iota(jnp.int32, (rows, rows), 0) > lax.broadcasted_iota(jnp.int32, (rows, rows), 1)
    earlier = jnp.dot(below.astype(jnp.bfloat16), counts, preferred_element_type=jnp.float32)
    keys = []
    for k in range(TOP):
        place = jnp.sum(earlier * named[k], axis=1, keepdims=True).astype(jnp.int32)
        keys.append(routes[:, k : k + 1] * capacity + place)
    return keys


def pack_kernel(experts, capacity, x_ref, gain_ref, routes_ref, out_ref, scale_ref, pick_ref):
    tile = out_ref.shape[1]
    step = pl.program_id(0)

    @pl.when(step == 0)
    def _():
        values = x_ref[...].astype(jnp.float32)
        scale_ref[...] = lax.rsqrt(jnp.mean(values * values, axis=-1, keepdims=True) + EPSILON)
        keys = slot_keys(routes_ref[...], experts, capacity)
        slots = lax.broadcasted_iota(jnp.int32, (x_ref.shape[0], experts * capacity), 1)
        taken = (keys[0] == slots) | (keys[1] == slots)
        pick_ref[...] = jnp.where(taken, 1.0, 0.0).astype(jnp.bfloat16)

    columns = pl.ds(pl.multiple_of(step * tile, tile), tile)
    values = x_ref[:, columns].astype(jnp.float32)
    normed = (values * scale_ref[...] * gain_ref[:, columns]).astype(jnp.bfloat16)
    out_ref[...] = lax.dot_general(
        pick_ref[...], normed, (((0,), (0,)), ((), ())), preferred_element_type=jnp.float32
    ).astype(jnp.bfloat16)


def pack(x, gain, routes, experts, capacity, tile=512):
    rows, width = x.shape
    slots = experts * capacity
    return pl.pallas_call(
        functools.partial(pack_kernel, experts, capacity),
        grid=(width // tile,),
        in_specs=[
            pl.BlockSpec((rows, width), lambda i: (0, 0)),
            pl.BlockSpec((1, width), lambda i: (0, 0)),
            pl.BlockSpec((rows, TOP), lambda i: (0, 0)),
        ],
        out_specs=pl.BlockSpec((slots, tile), lambda i: (0, i)),
        out_shape=jax.ShapeDtypeStruct((slots, width), jnp.bfloat16),
        scratch_shapes=[pltpu.VMEM((rows, 1), jnp.float32), pltpu.VMEM((rows, slots), jnp.bfloat16)],
        compiler_params=pltpu.CompilerParams(vmem_limit_bytes=VMEM_LIMIT),
        cost_estimate=pl.CostEstimate(flops=2 * rows * slots * width, bytes_accessed=2 * (rows + slots) * width, transcendentals=0),
        name="pack",
    )(x, gain, routes)


def mlp_kernel(up_tiles, rows_ref, gate_ref, up_ref, down_ref, out_ref, hidden_ref):
    step = pl.program_id(0)
    tile = gate_ref.shape[1]

    @pl.when(step < up_tiles)
    def _():
        rows = rows_ref[...]
        gate = jnp.dot(rows, gate_ref[...], preferred_element_type=jnp.float32)
        upward = jnp.dot(rows, up_ref[...], preferred_element_type=jnp.float32)
        columns = pl.ds(pl.multiple_of(step * tile, tile), tile)
        hidden_ref[:, columns] = (jax.nn.silu(gate) * upward).astype(jnp.bfloat16)

    @pl.when(step >= up_tiles)
    def _():
        out_ref[...] = jnp.dot(
            hidden_ref[...], down_ref[...], preferred_element_type=jnp.float32
        ).astype(jnp.bfloat16)


def mlp(rows, gate_matrix, up_matrix, down_matrix, up_tile=256, down_tile=512):
    slots, width = rows.shape
    inner = gate_matrix.shape[1]
    up_tiles, down_tiles = inner // up_tile, width // down_tile
    return pl.pallas_call(
        functools.partial(mlp_kernel, up_tiles),
        grid=(up_tiles + down_tiles,),
        in_specs=[
            pl.BlockSpec((slots, width), lambda i: (0, 0), pipeline_mode=pl.Buffered(1)),
            pl.BlockSpec((width, up_tile), lambda i: (0, jnp.minimum(i, up_tiles - 1))),
            pl.BlockSpec((width, up_tile), lambda i: (0, jnp.minimum(i, up_tiles - 1))),
            pl.BlockSpec((inner, down_tile), lambda i: (0, jnp.maximum(i - up_tiles, 0))),
        ],
        out_specs=pl.BlockSpec((slots, down_tile), lambda i: (0, jnp.maximum(i - up_tiles, 0))),
        out_shape=jax.ShapeDtypeStruct((slots, width), jnp.bfloat16),
        scratch_shapes=[pltpu.VMEM((slots, inner), jnp.bfloat16)],
        compiler_params=pltpu.CompilerParams(vmem_limit_bytes=VMEM_LIMIT),
        cost_estimate=pl.CostEstimate(
            flops=6 * slots * width * inner,
            bytes_accessed=2 * (2 * slots * width + 3 * width * inner),
            transcendentals=slots * inner,
        ),
        name="mlp",
    )(rows, gate_matrix, up_matrix, down_matrix)


def combine_kernel(experts, capacity, back_ref, x_ref, routes_ref, logits_ref, out_ref, weight_ref):
    rows = x_ref.shape[0]

    @pl.when(pl.program_id(0) == 0)
    def _():
        lifted = jax.nn.sigmoid(logits_ref[...])
        shares = lifted / jnp.sum(lifted, axis=-1, keepdims=True)
        keys = slot_keys(routes_ref[...], experts, capacity)
        slots = lax.broadcasted_iota(jnp.int32, (rows, experts * capacity), 1)
        weight = sum(jnp.where(keys[k] == slots, shares[:, k : k + 1], 0.0) for k in range(TOP))
        coarse = weight.astype(jnp.bfloat16)
        weight_ref[:rows, :] = coarse
        weight_ref[rows:, :] = (weight - coarse.astype(jnp.float32)).astype(jnp.bfloat16)

    mixed = jnp.dot(weight_ref[...], back_ref[...], preferred_element_type=jnp.float32)
    out_ref[...] = (x_ref[...].astype(jnp.float32) + (mixed[:rows] + mixed[rows:])).astype(jnp.bfloat16)


def combine(back, x, routes, logits, experts, capacity, tile=512):
    slots, width = back.shape
    rows = x.shape[0]
    return pl.pallas_call(
        functools.partial(combine_kernel, experts, capacity),
        grid=(width // tile,),
        in_specs=[
            pl.BlockSpec((slots, tile), lambda i: (0, i)),
            pl.BlockSpec((rows, tile), lambda i: (0, i)),
            pl.BlockSpec((rows, TOP), lambda i: (0, 0)),
            pl.BlockSpec((rows, TOP), lambda i: (0, 0)),
        ],
        out_specs=pl.BlockSpec((rows, tile), lambda i: (0, i)),
        out_shape=jax.ShapeDtypeStruct((rows, width), jnp.bfloat16),
        scratch_shapes=[pltpu.VMEM((2 * rows, slots), jnp.bfloat16)],
        compiler_params=pltpu.CompilerParams(vmem_limit_bytes=VMEM_LIMIT),
        cost_estimate=pl.CostEstimate(flops=4 * rows * slots * width, bytes_accessed=2 * (2 * rows + slots) * width, transcendentals=0),
        name="combine",
    )(back, x, routes, logits)


def exchange(blocks, experts, capacity):
    width = blocks.shape[1]
    moved = lax.all_to_all(blocks.reshape(experts, capacity, width), "expert", 0, 0, tiled=True)
    return moved.reshape(experts * capacity, width)


def shifted(value):
    count = lax.axis_size("section")
    return lax.ppermute(value, "section", [(i, (i + 1) % count) for i in range(count)])


def on_device(activations, norm_gain, w_gate, w_up, w_down, routes, gate_logits):
    experts = lax.axis_size("expert")
    capacity = 2 * activations.shape[1] * TOP // experts
    current = activations[0]
    for step in range(STEPS):
        chosen, logits = routes[step, 0], gate_logits[step, 0]
        packed = pack(current, norm_gain, chosen, experts, capacity)
        rows = exchange(packed, experts, capacity)
        produced = mlp(rows, w_gate[0, 0], w_up[0, 0], w_down[0, 0])
        back = exchange(produced, experts, capacity)
        current = shifted(combine(back, current, chosen, logits, experts, capacity))
    return current[None]


def solution(mesh):
    in_specs = (
        P("section", "expert", None),
        P("section", None),
        P("section", "expert", None, None),
        P("section", "expert", None, None),
        P("section", "expert", None, None),
        P(None, "section", "expert", None),
        P(None, "section", "expert", None),
    )
    return jax.shard_map(
        on_device, mesh=mesh, in_specs=in_specs, out_specs=P("section", "expert", None), check_vma=False
    )
```

time: 1040 us -> 308 us (0.30)
  waiting for transfers between devices: 737 us -> 118 us
  local copies, waits for them, and re-layouts: 159 us -> 5.47 us
  blocking collectives: 32.7 us -> 106 us
  Pallas kernels: 0 us -> 68.2 us
  matrix products: 52.1 us -> 0 us
  other arithmetic: 23.9 us -> 0 us
  between operations: 13.9 us -> 0.04 us
    all_gather x2 -> x0, waiting for transfers between devices: 609 us -> none  [on_device(): piece = lax.all_gather(normed[None], 'expert', axis=0, tiled=True)]
    all_to_all x2, blocking collectives: 32.7 us -> 106 us  [exchange(): lax.all_to_all(blocks.reshape(experts, capacity, width), 'expert', 0, 0,...]
    pallas_call x0 -> x6, Pallas kernels: none -> 68.2 us  [the longest x2 41.5 us: mlp(): pl.pallas_call(functools.partial(mlp_kernel, up_tiles), grid=(up_tiles +...]
    all_gather x2 -> x0, local copies, waits for them, and re-layouts: 55.4 us -> none  [on_device(): piece = lax.all_gather(normed[None], 'expert', axis=0, tiled=True)]
    gather x8 -> x0, local copies, waits for them, and re-layouts: 53 us -> none  [the longest x6 42 us: on_device(): collected = jax.vmap(lambda rows, index: rows[index])(extended, wanted)]
    dot_general x4 -> x0, matrix products: 52.1 us -> none  [the longest x2 33.1 us: expert_forward(): jnp.dot(hidden, down_matrix, preferred_element_type=jnp.float32)]
    concatenate x4 -> x0, local copies, waits for them, and re-layouts: 40.8 us -> none  [the longest x2 40.5 us: on_device(): jnp.concatenate([piece, jnp.zeros((piece.shape[0], 1, width), jnp.bfloat1...]
    reduce_sum x8 -> x0, other arithmetic: 17.8 us -> none  [the longest x2 14.7 us: on_device(): mixed = jnp.sum(shares[..., None] * fetched.astype(jnp.float32), axis=1)]
  transfers between devices with their start and end apart: 6 -> 4, of which waited for: 6 -> 4; matrix products, arithmetic and copies ran while one was open for 1% -> 1% of each run, Pallas kernels for 0% -> 0%
where the time goes in v1:
time: 308 us; the launch traced here: 307 us
  waiting for transfers between devices  118 us (38%)
  blocking collectives  106 us (34%)
  Pallas kernels  68.2 us (22%)
  starting transfers between devices  9.81 us (3%)
  local copies, waits for them, and re-layouts  5.47 us (2%)
    all_to_all x2, blocking collectives, exchange(): lax.all_to_all(blocks.reshape(experts, capacity, width), 'expert', 0, 0,...  106 us
    all_to_all x2, waiting for transfers between devices, exchange(): lax.all_to_all(blocks.reshape(experts, capacity, width), 'expert', 0, 0,...  89.4 us
    pallas_call x2, Pallas kernels, mlp(): pl.pallas_call(functools.partial(mlp_kernel, up_tiles), grid=(up_tiles +...  41.5 us
    ppermute x2, waiting for transfers between devices, shifted(): lax.ppermute(value, 'section', [(i, (i + 1) % count) for i in range(count)])  28.3 us
    pallas_call x2, Pallas kernels, combine(): pl.pallas_call(functools.partial(combine_kernel, experts, capacity), grid...  13.9 us
    pallas_call x2, Pallas kernels, pack(): pl.pallas_call(functools.partial(pack_kernel, experts, capacity), grid=(w...  12.8 us
    all_to_all x2, starting transfers between devices, exchange(): lax.all_to_all(blocks.reshape(experts, capacity, width), 'expert', 0, 0,...  9.8 us
  transfers between devices with their start and end apart: 4, of which 4 were waited for; matrix products, arithmetic and copies ran while one was open for 1% of the time, Pallas kernels for 0%

profile of v1, /device:TPU:0, one launch (start us, length us, event | category | flops | bytes accessed | tf_op | source)
XLA Modules:
  0.0 307.2 jit_solution(3919077577910613132)
XLA Ops:
  0.0 0.7 fusion.1
  0.7 0.7 copy.12
  1.4 6.4 %pack.2 = bf16[512,3584]{1,0:T(8,128)(2,1)} custom-call(bf16[128,3584]{1,0:T(8,128)(2,1)} %bitcast.23, f32[1,3584]{1,0:T(1,128)} %gain_ref.3, s32[128,2]{1,0:T(8,128)} %bitcast.28), custom_call_target="tpu_custom_call" | custom-call | flops 469762048 | bytes 4587520 | tf_op jit(solution)/shard_map/pack/pallas_call | solution.py:54
  7.9 54.2 %all_to_all.20 = bf16[32,16,3584]{2,1,0:T(8,128)(2,1)} all-to-all(bf16[32,16,3584]{2,1,0:T(8,128)(2,1)} %bitcast.17), channel_id=1, replica_groups=mesh['section'=4,'expert'=32] {'expert'}, dimensions={0} | all-to-all | bytes 7340032 | tf_op jit(solution)/shard_map/all_to_all | solution.py:157
  62.0 20.7 %mlp.2 = bf16[512,3584]{1,0:T(8,128)(2,1)} custom-call(bf16[512,3584]{1,0:T(8,128)(2,1)} %bitcast.21, bf16[3584,1024]{1,0:T(8,128)(2,1)} %bitcast.32, bf16[3584,1024]{1,0:T(8,128)(2,1)} %bitcast.34, bf16[1024,3584]{1,0:T(8,128)(2,1)} %bitcast.36), custom_call_target="tpu_custom_call" | custom-call | flops 11274289152 | bytes 29360128 | tf_op jit(solution)/shard_map/mlp/pallas_call | solution.py:94
  82.8 5.0 %all-to-all-start.1 = ((bf16[32,16,3584]{2,1,0:T(8,128)(2,1)}), bf16[32,16,3584]{2,1,0:T(8,128)(2,1)}, u32[]{:S(2)}, u32[]{:S(2)}) async-start(bf16[32,16,3584]{2,1,0:T(8,128)(2,1)} %bitcast.19), calls=%async_computation.1 | async-start | bytes 7340032 | tf_op jit(solution)/shard_map/all_to_all | solution.py:157
  87.7 0.0 copy-done.1
  87.8 0.7 copy.13
  88.5 44.4 %all-to-all-done.1 = bf16[32,16,3584]{2,1,0:T(8,128)(2,1)} async-done(((bf16[32,16,3584]{2,1,0:T(8,128)(2,1)}), bf16[32,16,3584]{2,1,0:T(8,128)(2,1)}, u32[]{:S(2)}, u32[]{:S(2)}) %all-to-all-start.1) | async-done | bytes 3670048 | tf_op jit(solution)/shard_map/all_to_all | solution.py:157
  132.9 6.9 %combine.2 = bf16[128,3584]{1,0:T(8,128)(2,1)} custom-call(bf16[512,3584]{1,0:T(8,128)(2,1)} %bitcast.8.back_ref, bf16[128,3584]{1,0:T(8,128)(2,1)} %bitcast.24, s32[128,2]{1,0:T(8,128)} %bitcast.29, f32[128,2]{1,0:T(8,128)} %bitcast.31), custom_call_target="tpu_custom_call" | custom-call | flops 939524096 | bytes 5505024 | tf_op jit(solution)/shard_map/combine/pallas_call | solution.py:137
  139.8 0.0 collective-permute-start
  139.8 0.7 copy.14
  140.6 13.8 %collective-permute-done.x_ref = bf16[128,3584]{1,0:T(8,128)(2,1)S(1)} collective-permute-done((bf16[128,3584]{1,0:T(8,128)(2,1)}, bf16[128,3584]{1,0:T(8,128)(2,1)S(1)}, u32[]{:S(2)}, u32[]{:S(2)}) %collective-permute-start) | collective-permute-done | bytes 917536 | tf_op jit(solution)/shard_map/ppermute | solution.py:163
  154.4 0.9 copy-done
  155.3 6.4 %pack.3 = bf16[512,3584]{1,0:T(8,128)(2,1)} custom-call(bf16[128,3584]{1,0:T(8,128)(2,1)} %copy-done, f32[1,3584]{1,0:T(1,128)} %gain_ref.3, s32[128,2]{1,0:T(8,128)} %bitcast.26), custom_call_target="tpu_custom_call" | custom-call | flops 469762048 | bytes 4587520 | tf_op jit(solution)/shard_map/pack/pallas_call | solution.py:54
  161.7 51.8 %all_to_all.21 = bf16[32,16,3584]{2,1,0:T(8,128)(2,1)} all-to-all(bf16[32,16,3584]{2,1,0:T(8,128)(2,1)} %bitcast.18), channel_id=1, replica_groups=mesh['section'=4,'expert'=32] {'expert'}, dimensions={0} | all-to-all | bytes 7340032 | tf_op jit(solution)/shard_map/all_to_all | solution.py:157
  213.5 20.7 %mlp.3 = bf16[512,3584]{1,0:T(8,128)(2,1)} custom-call(bf16[512,3584]{1,0:T(8,128)(2,1)} %bitcast.22, bf16[3584,1024]{1,0:T(8,128)(2,1)} %bitcast.33, bf16[3584,1024]{1,0:T(8,128)(2,1)} %bitcast.35, bf16[1024,3584]{1,0:T(8,128)(2,1)} %bitcast.37), custom_call_target="tpu_custom_call" | custom-call | flops 11274289152 | bytes 29360128 | tf_op jit(solution)/shard_map/mlp/pallas_call | solution.py:94
  234.2 4.8 %all-to-all-start.3 = ((bf16[32,16,3584]{2,1,0:T(8,128)(2,1)}), bf16[32,16,3584]{2,1,0:T(8,128)(2,1)}, u32[]{:S(2)}, u32[]{:S(2)}) async-start(bf16[32,16,3584]{2,1,0:T(8,128)(2,1)} %bitcast.20), calls=%async_computation.3 | async-start | bytes 7340032 | tf_op jit(solution)/shard_map/all_to_all | solution.py:157
  239.1 0.7 copy.15
  239.8 45.0 %all-to-all-done.3 = bf16[32,16,3584]{2,1,0:T(8,128)(2,1)} async-done(((bf16[32,16,3584]{2,1,0:T(8,128)(2,1)}), bf16[32,16,3584]{2,1,0:T(8,128)(2,1)}, u32[]{:S(2)}, u32[]{:S(2)}) %all-to-all-start.3) | async-done | bytes 3670048 | tf_op jit(solution)/shard_map/all_to_all | solution.py:157
  284.8 6.9 %combine.3 = bf16[128,3584]{1,0:T(8,128)(2,1)} custom-call(bf16[512,3584]{1,0:T(8,128)(2,1)} %bitcast.14.back_ref, bf16[128,3584]{1,0:T(8,128)(2,1)} %copy-done, s32[128,2]{1,0:T(8,128)} %bitcast.27, f32[128,2]{1,0:T(8,128)} %bitcast.30), custom_call_target="tpu_custom_call" | custom-call | flops 939524096 | bytes 5505024 | tf_op jit(solution)/shard_map/combine/pallas_call | solution.py:137
  291.7 0.0 collective-permute-start.1
  291.7 14.5 %collective-permute-done.1 = bf16[128,3584]{1,0:T(8,128)(2,1)S(1)} collective-permute-done((bf16[128,3584]{1,0:T(8,128)(2,1)}, bf16[128,3584]{1,0:T(8,128)(2,1)S(1)}, u32[]{:S(2)}, u32[]{:S(2)}) %collective-permute-start.1) | collective-permute-done | bytes 917536 | tf_op jit(solution)/shard_map/ppermute | solution.py:163
  306.3 0.9 copy.17
  (3 shorter events, 0.0 us)
Async XLA Ops:
  82.8 5.0 %copy-start.1 = (f32[2,1,128,2]{2,3,1,0:T(2,128)S(1)}, f32[2,1,128,2]{2,3,1,0:T(2,128)}, u32[]{:S(2)}) copy-start(f32[2,1,128,2]{2,3,1,0:T(2,128)} %param.13) | copy-start | bytes 6148
  82.8 50.1 %all-to-all-start.1 = ((bf16[32,16,3584]{2,1,0:T(8,128)(2,1)}), bf16[32,16,3584]{2,1,0:T(8,128)(2,1)}, u32[]{:S(2)}, u32[]{:S(2)}) async-start(bf16[32,16,3584]{2,1,0:T(8,128)(2,1)} %bitcast.19), calls=%async_computation.1 | async-start | bytes 7340032 | tf_op jit(solution)/shard_map/all_to_all | solution.py:157
  139.8 14.5 %collective-permute-start = (bf16[128,3584]{1,0:T(8,128)(2,1)}, bf16[128,3584]{1,0:T(8,128)(2,1)S(1)}, u32[]{:S(2)}, u32[]{:S(2)}) collective-permute-start(bf16[128,3584]{1,0:T(8,128)(2,1)} %combine.2), channel_id=1, source_target_pairs={{0,32},{32,64},{64,96},{96,0},{1,33},{33,65},{65,97},{97,1},{2,34}... | collective-permute-start | bytes 2752520 | tf_op jit(solution)/shard_map/ppermute | solution.py:163
  154.4 0.9 copy-start
  234.2 50.6 %all-to-all-start.3 = ((bf16[32,16,3584]{2,1,0:T(8,128)(2,1)}), bf16[32,16,3584]{2,1,0:T(8,128)(2,1)}, u32[]{:S(2)}, u32[]{:S(2)}) async-start(bf16[32,16,3584]{2,1,0:T(8,128)(2,1)} %bitcast.20), calls=%async_computation.3 | async-start | bytes 7340032 | tf_op jit(solution)/shard_map/all_to_all | solution.py:157
  291.7 14.5 %collective-permute-start.1 = (bf16[128,3584]{1,0:T(8,128)(2,1)}, bf16[128,3584]{1,0:T(8,128)(2,1)S(1)}, u32[]{:S(2)}, u32[]{:S(2)}) collective-permute-start(bf16[128,3584]{1,0:T(8,128)(2,1)} %combine.3), channel_id=1, source_target_pairs={{0,32},{32,64},{64,96},{96,0},{1,33},{33,65},{65,97},{97,1},{2,34}... | collective-permute-start | bytes 2752520 | tf_op jit(solution)/shard_map/ppermute | solution.py:163

commit v2 on v1

v2 whole, which is shorter than its diff:
```python
import functools

import jax
import jax.numpy as jnp
from jax import lax
from jax.experimental import pallas as pl
from jax.experimental.pallas import tpu as pltpu
from jax.sharding import PartitionSpec as P

TOP = 2
STEPS = 2
EPSILON = 1e-06
VMEM_LIMIT = 56 * 1024 * 1024
PARAMS = pltpu.CompilerParams(vmem_limit_bytes=VMEM_LIMIT)
ANY = pl.BlockSpec(memory_space=pl.ANY)
VMEM = pl.BlockSpec(memory_space=pltpu.VMEM)


def slot_rows(routes, experts, capacity):
    rows = routes.shape[1]
    lines = lax.broadcasted_iota(jnp.int32, (experts, rows), 0)
    named = [(routes[k : k + 1] == lines).astype(jnp.float32) for k in range(TOP)]
    counts = sum(named).astype(jnp.bfloat16)
    before = lax.broadcasted_iota(jnp.int32, (rows, rows), 0) < lax.broadcasted_iota(jnp.int32, (rows, rows), 1)
    earlier = jnp.dot(counts, jnp.where(before, 1.0, 0.0).astype(jnp.bfloat16), preferred_element_type=jnp.float32)
    return [
        routes[k : k + 1] * capacity + jnp.sum(earlier * named[k], axis=0, keepdims=True).astype(jnp.int32)
        for k in range(TOP)
    ]


def cuts(total, size):
    return [(start, min(size, total - start)) for start in range(0, total, size)]


def pack_kernel(experts, capacity, tile, x_ref, gain_ref, routes_ref, out_ref, held_ref, sems):
    rows, width = x_ref.shape
    slots = experts * capacity
    keys = slot_rows(routes_ref[...], experts, capacity)
    lines = lax.broadcasted_iota(jnp.int32, (slots, rows), 0)
    pick = jnp.where((keys[0] == lines) | (keys[1] == lines), 1.0, 0.0).astype(jnp.bfloat16)
    values = x_ref[...].astype(jnp.float32)
    scale = lax.rsqrt(jnp.mean(values * values, axis=-1, keepdims=True) + EPSILON)
    copies = []
    for i, (start, size) in enumerate(cuts(width, tile)):
        part = x_ref[:, start : start + size].astype(jnp.float32)
        normed = (part * scale * gain_ref[:, start : start + size]).astype(jnp.bfloat16)
        held_ref[:, start : start + size] = jnp.dot(pick, normed, preferred_element_type=jnp.float32).astype(jnp.bfloat16)
        copy = pltpu.make_async_copy(held_ref.at[:, start : start + size], out_ref.at[:, start : start + size], sems.at[i])
        copy.start()
        copies.append(copy)
    for copy in copies:
        copy.wait()


def pack(x, gain, routes, experts, capacity, tile=512):
    rows, width = x.shape
    slots = experts * capacity
    return pl.pallas_call(
        functools.partial(pack_kernel, experts, capacity, tile),
        in_specs=[VMEM, VMEM, VMEM],
        out_specs=ANY,
        out_shape=jax.ShapeDtypeStruct((slots, width), jnp.bfloat16),
        scratch_shapes=[pltpu.VMEM((slots, width), jnp.bfloat16), pltpu.SemaphoreType.DMA((len(cuts(width, tile)),))],
        compiler_params=PARAMS,
        cost_estimate=pl.CostEstimate(flops=2 * rows * slots * width, bytes_accessed=2 * (rows + slots) * width, transcendentals=0),
        name="pack",
    )(x, gain, routes)


def mlp_kernel(first_cut, in_tile, down_cuts, rows_hbm, gate_hbm, up_hbm, down_hbm, out_hbm,
               rows_ref, in_ref, total_ref, down_ref, hidden_ref, out_ref, row_sems, in_sems, down_sems, out_sems):
    width, inner = gate_hbm.shape
    first = cuts(width, first_cut)
    tiles = inner // in_tile

    def in_copies(tile, start, size, i):
        lines = pl.ds(start, size)
        place = 2 * in_tile * tile
        return [
            pltpu.make_async_copy(
                source.at[lines, pl.ds(tile * in_tile, in_tile)],
                in_ref.at[lines, pl.ds(place + k * in_tile, in_tile)],
                in_sems.at[2 * i + k],
            )
            for k, source in enumerate((gate_hbm, up_hbm))
        ]

    opening = []
    for i, (start, size) in enumerate(first):
        row_copy = pltpu.make_async_copy(rows_hbm.at[:, pl.ds(start, size)], rows_ref.at[:, pl.ds(start, size)], row_sems.at[i])
        opening.append([row_copy, *in_copies(0, start, size, i)])
    later = [in_copies(t, 0, width, len(first) + t - 1) for t in range(1, tiles)]
    later += [
        [pltpu.make_async_copy(down_hbm.at[:, pl.ds(start, size)], down_ref.at[:, pl.ds(start, size)], down_sems.at[i])]
        for i, (start, size) in enumerate(down_cuts)
    ]

    def begin(group):
        for copy in group:
            copy.start()

    def finish(group):
        for copy in group:
            copy.wait()

    for group in opening:
        begin(group)
    ahead = 2
    for group in later[:ahead]:
        begin(group)

    def activate(tile, both):
        gate, upward = both[:, :in_tile], both[:, in_tile:]
        hidden_ref[:, tile * in_tile : (tile + 1) * in_tile] = (jax.nn.silu(gate) * upward).astype(jnp.bfloat16)

    for i, (start, size) in enumerate(first):
        finish(opening[i])
        part = jnp.dot(rows_ref[:, start : start + size], in_ref[start : start + size, : 2 * in_tile], preferred_element_type=jnp.float32)
        if i == 0:
            total_ref[...] = part
        else:
            total_ref[...] += part
    activate(0, total_ref[...])
    for tile in range(1, tiles):
        if tile - 1 + ahead < len(later):
            begin(later[tile - 1 + ahead])
        finish(later[tile - 1])
        place = 2 * in_tile * tile
        activate(tile, jnp.dot(rows_ref[...], in_ref[:, place : place + 2 * in_tile], preferred_element_type=jnp.float32))
    sent = []
    for i, (start, size) in enumerate(down_cuts):
        if tiles - 1 + i + ahead < len(later):
            begin(later[tiles - 1 + i + ahead])
        finish(later[tiles - 1 + i])
        out_ref[:, start : start + size] = jnp.dot(
            hidden_ref[...], down_ref[:, start : start + size], preferred_element_type=jnp.float32
        ).astype(jnp.bfloat16)
        copy = pltpu.make_async_copy(out_ref.at[:, pl.ds(start, size)], out_hbm.at[:, pl.ds(start, size)], out_sems.at[i])
        copy.start()
        sent.append(copy)
    finish(sent)


def mlp(rows, gate_matrix, up_matrix, down_matrix, first_cut=512, in_tile=512, down_tile=1024):
    slots, width = rows.shape
    inner = gate_matrix.shape[1]
    down_cuts = cuts(width, down_tile)
    first, tiles = len(cuts(width, first_cut)), inner // in_tile
    dma = pltpu.SemaphoreType.DMA
    return pl.pallas_call(
        functools.partial(mlp_kernel, first_cut, in_tile, down_cuts),
        in_specs=[ANY] * 4,
        out_specs=ANY,
        out_shape=jax.ShapeDtypeStruct((slots, width), jnp.bfloat16),
        scratch_shapes=[
            pltpu.VMEM((slots, width), jnp.bfloat16),
            pltpu.VMEM((width, 2 * inner), jnp.bfloat16),
            pltpu.VMEM((slots, 2 * in_tile), jnp.float32),
            pltpu.VMEM((inner, width), jnp.bfloat16),
            pltpu.VMEM((slots, inner), jnp.bfloat16),
            pltpu.VMEM((slots, width), jnp.bfloat16),
            dma((first,)),
            dma((2 * (first + tiles - 1),)),
            dma((len(down_cuts),)),
            dma((len(down_cuts),)),
        ],
        compiler_params=PARAMS,
        cost_estimate=pl.CostEstimate(
            flops=6 * slots * width * inner,
            bytes_accessed=2 * (2 * slots * width + 3 * width * inner),
            transcendentals=slots * inner,
        ),
        name="mlp",
    )(rows, gate_matrix, up_matrix, down_matrix)


def combine_kernel(experts, capacity, tile, back_hbm, x_hbm, routes_ref, logits_ref, out_hbm, back_ref, x_ref, out_ref, sems, out_sems):
    rows, width = x_ref.shape
    slots = experts * capacity
    copies = []
    for i, (start, size) in enumerate(cuts(width, tile)):
        copy = pltpu.make_async_copy(back_hbm.at[:, pl.ds(start, size)], back_ref.at[:, pl.ds(start, size)], sems.at[i])
        copy.start()
        copies.append(copy)
        if i == 0:
            x_copy = pltpu.make_async_copy(x_hbm, x_ref, sems.at[len(cuts(width, tile))])
            x_copy.start()
    lifted = jax.nn.sigmoid(logits_ref[...])
    shares = lifted / jnp.sum(lifted, axis=0, keepdims=True)
    keys = slot_rows(routes_ref[...], experts, capacity)
    lines = lax.broadcasted_iota(jnp.int32, (slots, rows), 0)
    weight = sum(jnp.where(keys[k] == lines, shares[k : k + 1], 0.0) for k in range(TOP)).T
    coarse = weight.astype(jnp.bfloat16)
    fine = (weight - coarse.astype(jnp.float32)).astype(jnp.bfloat16)
    both = jnp.concatenate([coarse, fine], axis=0)
    x_copy.wait()
    sent = []
    for i, (start, size) in enumerate(cuts(width, tile)):
        copies[i].wait()
        mixed = jnp.dot(both, back_ref[:, start : start + size], preferred_element_type=jnp.float32)
        out_ref[:, start : start + size] = (
            x_ref[:, start : start + size].astype(jnp.float32) + (mixed[:rows] + mixed[rows:])
        ).astype(jnp.bfloat16)
        copy = pltpu.make_async_copy(out_ref.at[:, pl.ds(start, size)], out_hbm.at[:, pl.ds(start, size)], out_sems.at[i])
        copy.start()
        sent.append(copy)
    for copy in sent:
        copy.wait()


def combine(back, x, routes, logits, experts, capacity, tile=896):
    slots, width = back.shape
    rows = x.shape[0]
    return pl.pallas_call(
        functools.partial(combine_kernel, experts, capacity, tile),
        in_specs=[ANY, ANY, VMEM, VMEM],
        out_specs=ANY,
        out_shape=jax.ShapeDtypeStruct((rows, width), jnp.bfloat16),
        scratch_shapes=[
            pltpu.VMEM((slots, width), jnp.bfloat16),
            pltpu.VMEM((rows, width), jnp.bfloat16),
            pltpu.VMEM((rows, width), jnp.bfloat16),
            pltpu.SemaphoreType.DMA((len(cuts(width, tile)) + 1,)),
            pltpu.SemaphoreType.DMA((len(cuts(width, tile)),)),
        ],
        compiler_params=PARAMS,
        cost_estimate=pl.CostEstimate(flops=4 * rows * slots * width, bytes_accessed=2 * (2 * rows + slots) * width, transcendentals=0),
        name="combine",
    )(back, x, routes, logits)


def exchange(blocks, experts, capacity):
    width = blocks.shape[1]
    moved = lax.all_to_all(blocks.reshape(experts, capacity, width), "expert", 0, 0, tiled=True)
    return moved.reshape(experts * capacity, width)


def moved_from(value, odd):
    count = lax.axis_size("section")
    return lax.ppermute(value, "section", [(i, (i + 1) % count) for i in range(count) if i % 2 == odd])


def on_device(activations, norm_gain, w_gate, w_up, w_down, routes, gate_logits):
    experts = lax.axis_size("expert")
    capacity = 2 * activations.shape[1] * TOP // experts
    chosen = [routes[step, 0].T for step in range(STEPS)]
    logits = [gate_logits[step, 0].T for step in range(STEPS)]

    def layer(step, current):
        packed = pack(current, norm_gain, chosen[step], experts, capacity)
        rows = exchange(packed, experts, capacity)
        produced = mlp(rows, w_gate[0, 0], w_up[0, 0], w_down[0, 0])
        back = exchange(produced, experts, capacity)
        return combine(back, current, chosen[step], logits[step], experts, capacity)

    odd = lax.axis_index("section") % 2 == 1
    first = layer(0, activations[0])
    near, far = moved_from(first, 0), moved_from(first, 1)
    early = lax.cond(odd, lambda: layer(1, near), lambda: jnp.zeros_like(first))
    far_out = moved_from(early, 1)
    late = lax.cond(odd, lambda: jnp.zeros_like(first), lambda: layer(1, far))
    near_out = moved_from(late, 0)
    return jnp.where(odd, near_out, far_out)[None]


def solution(mesh):
    in_specs = (
        P("section", "expert", None),
        P("section", None),
        P("section", "expert", None, None),
        P("section", "expert", None, None),
        P("section", "expert", None, None),
        P(None, "section", "expert", None),
        P(None, "section", "expert", None),
    )
    return jax.shard_map(
        on_device, mesh=mesh, in_specs=in_specs, out_specs=P("section", "expert", None), check_vma=False
    )
```

time: 308 us -> 261 us (0.85)
  waiting for transfers between devices: 118 us -> 64.9 us
  blocking collectives: 106 us -> 135 us
  Pallas kernels: 68.2 us -> 45.3 us
  local copies, waits for them, and re-layouts: 5.47 us -> 1.94 us
    all_to_all x2 -> x1, waiting for transfers between devices: 89.4 us -> 44.5 us  [exchange(): lax.all_to_all(blocks.reshape(experts, capacity, width), 'expert', 0, 0,...]
    all_to_all x2 -> x3, blocking collectives: 106 us -> 135 us  [exchange(): lax.all_to_all(blocks.reshape(experts, capacity, width), 'expert', 0, 0,...]
    pallas_call x6, Pallas kernels: 68.2 us -> 45.3 us  [the longest x2 31.3 us: mlp(): pl.pallas_call(functools.partial(mlp_kernel, first_cut, in_tile, down_cut...]
    ppermute x2 -> x4, waiting for transfers between devices: 28.3 us -> 20.4 us  [moved_from(): lax.ppermute(value, 'section', [(i, (i + 1) % count) for i in range(count...]
    ppermute x2 -> x4, starting transfers between devices: 0.01 us -> 5.28 us  [moved_from(): lax.ppermute(value, 'section', [(i, (i + 1) % count) for i in range(count...]
    all_to_all x2 -> x1, starting transfers between devices: 9.8 us -> 4.85 us  [exchange(): lax.all_to_all(blocks.reshape(experts, capacity, width), 'expert', 0, 0,...]
    unnamed x9 -> x6, local copies, waits for them, and re-layouts: 4.77 us -> 0.02 us
  transfers between devices with their start and end apart: 4 -> 5, of which waited for: 4 -> 4; matrix products, arithmetic and copies ran while one was open for 1% -> 0% of each run, Pallas kernels for 0% -> 8%
where the time goes in v2:
time: 261 us; the launch traced here: 260 us
  blocking collectives  135 us (52%)
  waiting for transfers between devices  64.9 us (25%)
  Pallas kernels  45.3 us (17%)
  starting transfers between devices  10.1 us (4%)
    all_to_all x3, blocking collectives, exchange(): lax.all_to_all(blocks.reshape(experts, capacity, width), 'expert', 0, 0,...  135 us
    all_to_all x1, waiting for transfers between devices, exchange(): lax.all_to_all(blocks.reshape(experts, capacity, width), 'expert', 0, 0,...  44.5 us
    pallas_call x2, Pallas kernels, mlp(): pl.pallas_call(functools.partial(mlp_kernel, first_cut, in_tile, down_cut...  31.3 us
    ppermute x4, waiting for transfers between devices, moved_from(): lax.ppermute(value, 'section', [(i, (i + 1) % count) for i in range(count...  20.4 us
    pallas_call x2, Pallas kernels, combine(): pl.pallas_call(functools.partial(combine_kernel, experts, capacity, tile)...  7.83 us
    pallas_call x2, Pallas kernels, pack(): pl.pallas_call(functools.partial(pack_kernel, experts, capacity, tile), i...  6.19 us
    ppermute x4, starting transfers between devices, moved_from(): lax.ppermute(value, 'section', [(i, (i + 1) % count) for i in range(count...  5.28 us
  transfers between devices with their start and end apart: 5, of which 4 were waited for; matrix products, arithmetic and copies ran while one was open for 0% of the time, Pallas kernels for 8%

profile of v2, /device:TPU:0, one launch (start us, length us, event | category | flops | bytes accessed | tf_op | source)
XLA Modules:
  0.0 259.5 jit_solution(13262405067056144193)
XLA Ops:
  0.0 1.3 slice_bitcast_fusion.1
  1.3 3.7 %pack.5 = bf16[512,3584]{1,0:T(8,128)(2,1)} custom-call(bf16[128,3584]{1,0:T(8,128)(2,1)} %bitcast.51, f32[1,3584]{1,0:T(1,128)} %gain_ref.1, s32[2,128]{1,0:T(2,128)} %get-tuple-element.56.routes_ref), custom_call_target="tpu_custom_call" | custom-call | flops 469762048 | bytes 4587520 | tf_op jit(solution)/shard_map/pack/pallas_call | solution.py:59
  5.0 54.4 %all_to_all.30 = bf16[32,16,3584]{2,1,0:T(8,128)(2,1)} all-to-all(bf16[32,16,3584]{2,1,0:T(8,128)(2,1)} %bitcast.42), channel_id=1, replica_groups=mesh['section'=4,'expert'=32] {'expert'}, dimensions={0} | all-to-all | bytes 7340032 | tf_op jit(solution)/shard_map/all_to_all | solution.py:235
  59.4 15.0 %mlp.5 = bf16[512,3584]{1,0:T(8,128)(2,1)} custom-call(bf16[512,3584]{1,0:T(8,128)(2,1)} %bitcast.46, bf16[3584,1024]{1,0:T(8,128)(2,1)S(1)} %bitcast.53, bf16[3584,1024]{1,0:T(8,128)(2,1)} %bitcast.56, bf16[1024,3584]{1,0:T(8,128)(2,1)} %bitcast.59), custom_call_target="tpu_custom_call" | custom-call | flops 11274289152 | bytes 29360128 | tf_op jit(solution)/shard_map/mlp/pallas_call | solution.py:151
  74.5 4.8 %all-to-all-start.5 = ((bf16[32,16,3584]{2,1,0:T(8,128)(2,1)}), bf16[32,16,3584]{2,1,0:T(8,128)(2,1)}, u32[]{:S(2)}, u32[]{:S(2)}) async-start(bf16[32,16,3584]{2,1,0:T(8,128)(2,1)} %bitcast.45), calls=%async_computation.5 | async-start | bytes 7340032 | tf_op jit(solution)/shard_map/all_to_all | solution.py:235
  79.4 0.6 slice_bitcast_fusion
  80.0 44.5 %all-to-all-done.5 = bf16[32,16,3584]{2,1,0:T(8,128)(2,1)} async-done(((bf16[32,16,3584]{2,1,0:T(8,128)(2,1)}), bf16[32,16,3584]{2,1,0:T(8,128)(2,1)}, u32[]{:S(2)}, u32[]{:S(2)}) %all-to-all-start.5) | async-done | bytes 3670048 | tf_op jit(solution)/shard_map/all_to_all | solution.py:235
  124.5 4.7 %combine.5 = bf16[128,3584]{1,0:T(8,128)(2,1)} custom-call(bf16[512,3584]{1,0:T(8,128)(2,1)} %bitcast.23.back_hbm, bf16[128,3584]{1,0:T(8,128)(2,1)} %bitcast.52, s32[2,128]{1,0:T(2,128)} %get-tuple-element.56.routes_ref, f32[2,128]{1,0:T(2,128)} %get-tuple-element.54.logits_ref), custom_call_target="tpu_custom_call" | custom-call | flops 939524096 | bytes 5505024 | tf_op jit(solution)/shard_map/combine/pallas_call | solution.py:215
  129.2 1.3 collective-permute-start.2
  130.6 1.3 collective-permute-start
  131.9 0.9 collective-permute-done.2
  132.8 0.3 conditional.3
  132.8 0.1 broadcast.6
  133.1 1.3 collective-permute-start.3
  134.4 12.6 %collective-permute-done = bf16[128,3584]{1,0:T(8,128)(2,1)S(1)} collective-permute-done((bf16[128,3584]{1,0:T(8,128)(2,1)}, bf16[128,3584]{1,0:T(8,128)(2,1)S(1)}, u32[]{:S(2)}, u32[]{:S(2)}) %collective-permute-start) | collective-permute-done | bytes 917536 | tf_op jit(solution)/shard_map/ppermute | solution.py:241
  147.0 102.1 %conditional.2 = (bf16[128,3584]{1,0:T(8,128)(2,1)S(1)}) conditional(s32[]{:T(128)} %convert_element_type.4, (bf16[128,3584]{1,0:T(8,128)(2,1)S(1)}, f32[1,3584]{1,0:T(1,128)S(1)}, s32[2,128]{1,0:T(2,128)S(1)}, bf16[1,1,3584,1024]{3,2,1,0:T(8,128)(2,1)}, bf16[1,1,3584,1024]{3,2,1,0:T(8,128)(2,1)}, /*index=5*/bf16[1,1,1024,3584]{3,2,1,0:T(8,128)(2,1)}, ...), branch_computations={%region_0.1_spmd, %region_1.2_spmd} | conditional | flops 12683575296 | bytes 54132744 | solution.py:262
  147.0 2.5 pack.3
  149.5 48.3 %all_to_all.26 = bf16[32,16,3584]{2,1,0:T(8,128)(2,1)} all-to-all(bf16[32,16,3584]{2,1,0:T(8,128)(2,1)} %bitcast.44), channel_id=1, replica_groups=mesh['section'=4,'expert'=32] {'expert'}, dimensions={0} | all-to-all | bytes 7340032 | tf_op jit(solution)/shard_map/cond/branch_0_fun/all_to_all | solution.py:235
  197.7 16.3 %mlp.3 = bf16[512,3584]{1,0:T(8,128)(2,1)} custom-call(bf16[512,3584]{1,0:T(8,128)(2,1)} %bitcast.49, bf16[3584,1024]{1,0:T(8,128)(2,1)} %bitcast.55, bf16[3584,1024]{1,0:T(8,128)(2,1)} %bitcast.58, bf16[1024,3584]{1,0:T(8,128)(2,1)} %bitcast.61), custom_call_target="tpu_custom_call" | custom-call | flops 11274289152 | bytes 29360128 | tf_op jit(solution)/shard_map/cond/branch_0_fun/mlp/pallas_call | solution.py:151
  214.0 31.9 %all_to_all.27 = bf16[32,16,3584]{2,1,0:T(8,128)(2,1)} all-to-all(bf16[32,16,3584]{2,1,0:T(8,128)(2,1)} %bitcast.50), channel_id=1, replica_groups=mesh['section'=4,'expert'=32] {'expert'}, dimensions={0} | all-to-all | bytes 7340032 | tf_op jit(solution)/shard_map/cond/branch_0_fun/all_to_all | solution.py:235
  245.9 3.1 %combine.3 = bf16[128,3584]{1,0:T(8,128)(2,1)S(1)} custom-call(bf16[512,3584]{1,0:T(8,128)(2,1)} %bitcast.41, bf16[128,3584]{1,0:T(8,128)(2,1)S(1)} %get-tuple-element.38.x_ref.x_hbm, s32[2,128]{1,0:T(2,128)S(1)} %get-tuple-element.41.routes_ref, f32[2,128]{1,0:T(2,128)S(1)} %get-tuple-element.45.logits_ref), custom_call_target="tpu_custom_call" | custom-call | flops 939524096 | bytes 5505024 | tf_op jit(solution)/shard_map/cond/branch_0_fun/combine/pallas_call | solution.py:215
  249.1 1.3 collective-permute-start.1
  250.4 6.9 %collective-permute-done.3 = bf16[128,3584]{1,0:T(8,128)(2,1)} collective-permute-done((bf16[128,3584]{1,0:T(8,128)(2,1)S(1)}, bf16[128,3584]{1,0:T(8,128)(2,1)}, u32[]{:S(2)}, u32[]{:S(2)}) %collective-permute-start.3) | collective-permute-done | bytes 917536 | tf_op jit(solution)/shard_map/ppermute | solution.py:241
  257.3 2.2 select_bitcast_fusion
  (7 shorter events, 0.0 us)
Async XLA Ops:
  5.0 54.5 %copy-start.2 = (bf16[1,1,3584,1024]{3,2,1,0:T(8,128)(2,1)S(1)}, bf16[1,1,3584,1024]{3,2,1,0:T(8,128)(2,1)}, u32[]{:S(2)}) copy-start(bf16[1,1,3584,1024]{3,2,1,0:T(8,128)(2,1)} %param.13) | copy-start | bytes 22020100
  74.5 4.9 %copy-start.1 = (f32[2,1,128,2]{2,3,1,0:T(2,128)S(1)}, f32[2,1,128,2]{2,3,1,0:T(2,128)}, u32[]{:S(2)}) copy-start(f32[2,1,128,2]{2,3,1,0:T(2,128)} %param.17) | copy-start | bytes 6148
  74.5 50.0 %all-to-all-start.5 = ((bf16[32,16,3584]{2,1,0:T(8,128)(2,1)}), bf16[32,16,3584]{2,1,0:T(8,128)(2,1)}, u32[]{:S(2)}, u32[]{:S(2)}) async-start(bf16[32,16,3584]{2,1,0:T(8,128)(2,1)} %bitcast.45), calls=%async_computation.5 | async-start | bytes 7340032 | tf_op jit(solution)/shard_map/all_to_all | solution.py:235
  79.4 53.4 %copy-start = (f32[1,3584]{1,0:T(1,128)S(1)}, f32[1,3584]{1,0:T(1,128)}, u32[]{:S(2)}) copy-start(f32[1,3584]{1,0:T(1,128)} %gain_ref.1) | copy-start | bytes 43012
  129.2 3.6 %collective-permute-start.2 = (bf16[128,3584]{1,0:T(8,128)(2,1)}, bf16[128,3584]{1,0:T(8,128)(2,1)S(1)}, u32[]{:S(2)}, u32[]{:S(2)}) collective-permute-start(bf16[128,3584]{1,0:T(8,128)(2,1)} %combine.5), channel_id=1, source_target_pairs={{0,32},{64,96},{1,33},{65,97},{2,34},{66,98},{3,35},{67,99},{4,36}... | collective-permute-start | bytes 2752520 | tf_op jit(solution)/shard_map/ppermute | solution.py:241
  130.6 16.4 %collective-permute-start = (bf16[128,3584]{1,0:T(8,128)(2,1)}, bf16[128,3584]{1,0:T(8,128)(2,1)S(1)}, u32[]{:S(2)}, u32[]{:S(2)}) collective-permute-start(bf16[128,3584]{1,0:T(8,128)(2,1)} %combine.5), channel_id=1, source_target_pairs={{32,64},{96,0},{33,65},{97,1},{34,66},{98,2},{35,67},{99,3},{36,68... | collective-permute-start | bytes 2752520 | tf_op jit(solution)/shard_map/ppermute | solution.py:241
  133.1 124.2 %collective-permute-start.3 = (bf16[128,3584]{1,0:T(8,128)(2,1)S(1)}, bf16[128,3584]{1,0:T(8,128)(2,1)}, u32[]{:S(2)}, u32[]{:S(2)}) collective-permute-start(bf16[128,3584]{1,0:T(8,128)(2,1)S(1)} %get-tuple-element.58), channel_id=1, source_target_pairs={{32,64},{96,0},{33,65},{97,1},{34,66},{98,2},{35,67},{99,3},{36,68... | collective-permute-start | bytes 2752520 | tf_op jit(solution)/shard_map/ppermute | solution.py:241
  249.1 8.2 %collective-permute-start.1 = (bf16[128,3584]{1,0:T(8,128)(2,1)S(1)}, bf16[128,3584]{1,0:T(8,128)(2,1)S(1)}, u32[]{:S(2)}, u32[]{:S(2)}) collective-permute-start(bf16[128,3584]{1,0:T(8,128)(2,1)S(1)} %get-tuple-element.57), channel_id=1, source_target_pairs={{0,32},{64,96},{1,33},{65,97},{2,34},{66,98},{3,35},{67,99},{4,36}... | collective-permute-start | bytes 2752520 | tf_op jit(solution)/shard_map/ppermute | solution.py:241

commit v3 on v2

v3 whole, which is shorter than its diff:
```python
import functools

import jax
import jax.numpy as jnp
from jax import lax
from jax.experimental import pallas as pl
from jax.experimental.pallas import tpu as pltpu
from jax.sharding import PartitionSpec as P

TOP = 2
STEPS = 2
EPSILON = 1e-06
VMEM_LIMIT = 56 * 1024 * 1024
PARAMS = pltpu.CompilerParams(vmem_limit_bytes=VMEM_LIMIT)
ANY = pl.BlockSpec(memory_space=pl.ANY)
VMEM = pl.BlockSpec(memory_space=pltpu.VMEM)


def slot_rows(routes, experts, capacity):
    rows = routes.shape[1]
    lines = lax.broadcasted_iota(jnp.int32, (experts, rows), 0)
    named = [(routes[k : k + 1] == lines).astype(jnp.float32) for k in range(TOP)]
    counts = sum(named).astype(jnp.bfloat16)
    before = lax.broadcasted_iota(jnp.int32, (rows, rows), 0) < lax.broadcasted_iota(jnp.int32, (rows, rows), 1)
    earlier = jnp.dot(counts, jnp.where(before, 1.0, 0.0).astype(jnp.bfloat16), preferred_element_type=jnp.float32)
    return [
        routes[k : k + 1] * capacity + jnp.sum(earlier * named[k], axis=0, keepdims=True).astype(jnp.int32)
        for k in range(TOP)
    ]


def cuts(total, size):
    return [(start, min(size, total - start)) for start in range(0, total, size)]


def pack_kernel(step, experts, capacity, tile, widths, *refs):
    if widths:
        flag_ref, x_ref, gain_ref, routes_ref, whole_hbm, *parts, held_ref, sems = refs
    else:
        x_ref, gain_ref, routes_ref, whole_hbm, held_ref, sems = refs
        parts = []
    rows, width = x_ref.shape
    slots = experts * capacity
    keys = slot_rows(routes_ref[step], experts, capacity)
    lines = lax.broadcasted_iota(jnp.int32, (slots, rows), 0)
    pick = jnp.where((keys[0] == lines) | (keys[1] == lines), 1.0, 0.0).astype(jnp.bfloat16)
    values = x_ref[...].astype(jnp.float32)
    scale = lax.rsqrt(jnp.mean(values * values, axis=-1, keepdims=True) + EPSILON)
    targets = [part.at[:, start : start + tile] for part, size in zip(parts, widths) for start in range(0, size, tile)]

    def each(i, start, size, act):
        source = held_ref.at[:, start : start + size]
        whole = pltpu.make_async_copy(source, whole_hbm.at[:, start : start + size], sems.at[i])
        if targets:
            part = pltpu.make_async_copy(source, targets[i], sems.at[i])
            pl.when(flag_ref[0] == 0)(lambda: act(whole))
            pl.when(flag_ref[0] == 1)(lambda: act(part))
        else:
            act(whole)

    for i, (start, size) in enumerate(cuts(width, tile)):
        values = x_ref[:, start : start + size].astype(jnp.float32)
        normed = (values * scale * gain_ref[:, start : start + size]).astype(jnp.bfloat16)
        held_ref[:, start : start + size] = jnp.dot(pick, normed, preferred_element_type=jnp.float32).astype(jnp.bfloat16)
        each(i, start, size, lambda copy: copy.start())
    for i, (start, size) in enumerate(cuts(width, tile)):
        each(i, start, size, lambda copy: copy.wait())


def pack(step, x, gain, routes, experts, capacity, flag=None, widths=(), tile=512):
    rows, width = x.shape
    slots = experts * capacity
    shapes = [jax.ShapeDtypeStruct((slots, size), jnp.bfloat16) for size in (width, *widths)]
    flags = [flag] if widths else []
    out = pl.pallas_call(
        functools.partial(pack_kernel, step, experts, capacity, tile, widths),
        in_specs=[pl.BlockSpec(memory_space=pltpu.SMEM)] * len(flags) + [VMEM, VMEM, VMEM],
        out_specs=[ANY] * len(shapes),
        out_shape=shapes,
        scratch_shapes=[pltpu.VMEM((slots, width), jnp.bfloat16), pltpu.SemaphoreType.DMA((len(cuts(width, tile)),))],
        compiler_params=PARAMS,
        cost_estimate=pl.CostEstimate(flops=2 * rows * slots * width, bytes_accessed=2 * (rows + slots) * width, transcendentals=0),
        name="pack",
    )(*flags, x, gain, routes)
    return out if widths else out[0]


def mlp_kernel(widths, turn, depth, in_tile, down_tile, *refs):
    sources = refs[: len(widths)]
    gate_hbm, up_hbm, down_hbm, *_, out_hbm = refs[len(widths) : -11]
    rows_ref, in_ref, total_ref, down_ref, hidden_ref, out_ref, row_sems, first_sems, in_sems, down_sems, out_sems = refs[-11:]
    slots = rows_ref.shape[0]
    width, inner = gate_hbm.shape
    depths, tiles, downs = width // depth, inner // in_tile, width // down_tile

    def span(index, size):
        return pl.ds(pl.multiple_of(index * size, size), size)

    def first_copies(i):
        lines = span(i, depth)
        return [
            pltpu.make_async_copy(
                source.at[lines, pl.ds(0, in_tile)], in_ref.at[lines, pl.ds(k * in_tile, in_tile)], first_sems.at[k, i]
            )
            for k, source in enumerate((gate_hbm, up_hbm))
        ]

    def in_copies(tile):
        return [
            pltpu.make_async_copy(source.at[:, span(tile, in_tile)], in_ref.at[:, span(2 * tile + k, in_tile)], in_sems.at[k, tile])
            for k, source in enumerate((gate_hbm, up_hbm))
        ]

    def down_copies(i):
        return [pltpu.make_async_copy(down_hbm.at[:, span(i, down_tile)], down_ref.at[:, span(i, down_tile)], down_sems.at[i])]

    def out_copies(i):
        pieces = [(0, turn, slots - turn), (slots - turn, 0, turn)] if turn else [(0, 0, slots)]
        return [
            pltpu.make_async_copy(
                out_ref.at[pl.ds(source, lines), span(i, down_tile)],
                out_hbm.at[pl.ds(target, lines), span(i, down_tile)],
                out_sems.at[k, i],
            )
            for k, (source, target, lines) in enumerate(pieces)
        ]

    def begin(copies):
        for copy in copies:
            copy.start()

    def finish(copies):
        for copy in copies:
            copy.wait()

    def activate(tile, both):
        gate, upward = both[:, :in_tile], both[:, in_tile:]
        hidden_ref[:, span(tile, in_tile)] = (jax.nn.silu(gate) * upward).astype(jnp.bfloat16)

    places = [(source, start) for source, size in zip(sources, widths) for start in range(0, size, depth)]
    for i, (source, start) in enumerate(places):
        pltpu.make_async_copy(source.at[:, start : start + depth], rows_ref.at[:, span(i, depth)], row_sems.at[i]).start()
        begin(first_copies(i))
    begin(in_copies(1))

    def opening(i, carry):
        pltpu.make_async_copy(sources[0].at[:, :depth], rows_ref.at[:, span(i, depth)], row_sems.at[i]).wait()
        finish(first_copies(i))
        total_ref[...] = jnp.where(i == 0, 0.0, total_ref[...]) + jnp.dot(
            rows_ref[:, span(i, depth)], in_ref[span(i, depth), pl.ds(0, 2 * in_tile)], preferred_element_type=jnp.float32
        )
        return carry

    lax.fori_loop(0, depths, opening, 0)
    begin(in_copies(2))
    activate(0, total_ref[...])

    def inward(tile, carry):
        @pl.when(tile < tiles - 2)
        def _():
            begin(in_copies(tile + 2))

        @pl.when(tile >= tiles - 2)
        def _():
            begin(down_copies(2 * (tile - tiles + 2)))
            begin(down_copies(2 * (tile - tiles + 2) + 1))

        finish(in_copies(tile))
        activate(tile, jnp.dot(rows_ref[...], in_ref[:, span(tile, 2 * in_tile)], preferred_element_type=jnp.float32))
        return carry

    lax.fori_loop(1, tiles, inward, 0)

    def outward(i, carry):
        finish(down_copies(i))
        out_ref[:, span(i, down_tile)] = jnp.dot(
            hidden_ref[...], down_ref[:, span(i, down_tile)], preferred_element_type=jnp.float32
        ).astype(jnp.bfloat16)
        begin(out_copies(i))
        return carry

    lax.fori_loop(0, downs, outward, 0)
    for i in range(downs):
        finish(out_copies(i))


def mlp(rows, gate_matrix, up_matrix, down_matrix, *after, turn=0, depth=512, in_tile=256, down_tile=896):
    slots, width = rows[0].shape[0], gate_matrix.shape[0]
    widths = [part.shape[1] for part in rows]
    inner = gate_matrix.shape[1]
    depths, tiles, downs = width // depth, inner // in_tile, width // down_tile
    dma = pltpu.SemaphoreType.DMA
    return pl.pallas_call(
        functools.partial(mlp_kernel, widths, turn, depth, in_tile, down_tile),
        in_specs=[ANY] * (len(rows) + 3 + len(after)),
        out_specs=ANY,
        out_shape=jax.ShapeDtypeStruct((slots, width), jnp.bfloat16),
        scratch_shapes=[
            pltpu.VMEM((slots, width), jnp.bfloat16),
            pltpu.VMEM((width, 2 * inner), jnp.bfloat16),
            pltpu.VMEM((slots, 2 * in_tile), jnp.float32),
            pltpu.VMEM((inner, width), jnp.bfloat16),
            pltpu.VMEM((slots, inner), jnp.bfloat16),
            pltpu.VMEM((slots, width), jnp.bfloat16),
            dma((depths,)),
            dma((2, depths)),
            dma((2, tiles)),
            dma((downs,)),
            dma((2, downs)),
        ],
        compiler_params=PARAMS,
        cost_estimate=pl.CostEstimate(
            flops=6 * slots * width * inner,
            bytes_accessed=2 * (2 * slots * width + 3 * width * inner),
            transcendentals=slots * inner,
        ),
        name="mlp",
    )(*rows, gate_matrix, up_matrix, down_matrix, *after)


def combine_kernel(step, experts, capacity, tile, back_hbm, x_hbm, routes_ref, logits_ref, out_hbm, back_ref, x_ref, out_ref, sems, out_sems):
    rows, width = x_ref.shape
    slots = experts * capacity
    copies = []
    for i, (start, size) in enumerate(cuts(width, tile)):
        copy = pltpu.make_async_copy(back_hbm.at[:, pl.ds(start, size)], back_ref.at[:, pl.ds(start, size)], sems.at[i])
        copy.start()
        copies.append(copy)
        if i == 0:
            x_copy = pltpu.make_async_copy(x_hbm, x_ref, sems.at[len(cuts(width, tile))])
            x_copy.start()
    lifted = jax.nn.sigmoid(logits_ref[step])
    shares = lifted / jnp.sum(lifted, axis=0, keepdims=True)
    keys = slot_rows(routes_ref[step], experts, capacity)
    lines = lax.broadcasted_iota(jnp.int32, (slots, rows), 0)
    weight = sum(jnp.where(keys[k] == lines, shares[k : k + 1], 0.0) for k in range(TOP)).T
    coarse = weight.astype(jnp.bfloat16)
    fine = (weight - coarse.astype(jnp.float32)).astype(jnp.bfloat16)
    both = jnp.concatenate([coarse, fine], axis=0)
    x_copy.wait()
    sent = []
    for i, (start, size) in enumerate(cuts(width, tile)):
        copies[i].wait()
        mixed = jnp.dot(both, back_ref[:, start : start + size], preferred_element_type=jnp.float32)
        out_ref[:, start : start + size] = (
            x_ref[:, start : start + size].astype(jnp.float32) + (mixed[:rows] + mixed[rows:])
        ).astype(jnp.bfloat16)
        copy = pltpu.make_async_copy(out_ref.at[:, pl.ds(start, size)], out_hbm.at[:, pl.ds(start, size)], out_sems.at[i])
        copy.start()
        sent.append(copy)
    for copy in sent:
        copy.wait()


def combine(step, back, x, routes, logits, experts, capacity, tile=896):
    slots, width = back.shape
    rows = x.shape[0]
    return pl.pallas_call(
        functools.partial(combine_kernel, step, experts, capacity, tile),
        in_specs=[ANY, ANY, VMEM, VMEM],
        out_specs=ANY,
        out_shape=jax.ShapeDtypeStruct((rows, width), jnp.bfloat16),
        scratch_shapes=[
            pltpu.VMEM((slots, width), jnp.bfloat16),
            pltpu.VMEM((rows, width), jnp.bfloat16),
            pltpu.VMEM((rows, width), jnp.bfloat16),
            pltpu.SemaphoreType.DMA((len(cuts(width, tile)) + 1,)),
            pltpu.SemaphoreType.DMA((len(cuts(width, tile)),)),
        ],
        compiler_params=PARAMS,
        cost_estimate=pl.CostEstimate(flops=4 * rows * slots * width, bytes_accessed=2 * (2 * rows + slots) * width, transcendentals=0),
        name="combine",
    )(back, x, routes, logits)
PARTS = (512, 3072)


def exchange(blocks, experts, capacity):
    width = blocks.shape[1]
    moved = lax.all_to_all(blocks.reshape(experts, capacity, width), "expert", 0, 0, tiled=True)
    return moved.reshape(experts * capacity, width)


def moved_from(value, odd, turn=0):
    sections, experts = lax.axis_size("section"), lax.axis_size("expert")
    pairs = [
        (i * experts + j, (i + 1) % sections * experts + (j + turn) % experts)
        for i in range(odd, sections, 2)
        for j in range(experts)
    ]
    return lax.ppermute(value, ("section", "expert"), pairs)


def on_device(activations, norm_gain, w_gate, w_up, w_down, routes, gate_logits):
    experts = lax.axis_size("expert")
    capacity = 2 * activations.shape[1] * TOP // experts
    chosen, logits = (value[:, 0].transpose(0, 2, 1) for value in (routes, gate_logits))
    start = activations[0]
    parity = lax.axis_index("section") % 2
    odd = parity == 1
    nothing = functools.partial(jnp.zeros_like, start)

    def spread(step, current):
        return exchange(pack(step, current, norm_gain, chosen, experts, capacity), experts, capacity)

    def gather(step, current, rows, *after):
        produced = mlp(rows, w_gate[0, 0], w_up[0, 0], w_down[0, 0], *after)
        back = exchange(produced, experts, capacity)
        return combine(step, back, current, chosen, logits, experts, capacity)

    flag = parity.astype(jnp.int32).reshape(1)
    whole, *parts = pack(0, start, norm_gain, chosen, experts, capacity, flag, PARTS)

    def in_turn():
        rows = []
        for part in parts:
            if rows:
                part, rows[-1] = lax.optimization_barrier((part, rows[-1]))
            rows.append(exchange(part, experts, capacity))
        return rows

    first_even = lax.cond(odd, nothing, lambda: gather(0, start, (exchange(whole, experts, capacity),)))
    near = moved_from(first_even, 0)
    first_odd = lax.cond(odd, lambda: gather(0, start, in_turn(), first_even), nothing)
    far = moved_from(first_odd, 1)
    early = lax.cond(odd, lambda: gather(1, near, (spread(1, near),)), nothing)
    far_out = moved_from(early, 1)
    late = lax.cond(odd, nothing, lambda: gather(1, far, (spread(1, far),), early))
    near_out = moved_from(late, 0)
    kept = lax.cond(odd, nothing, lambda: far_out + jnp.bfloat16(0))
    return jnp.where(parity == 0, kept, near_out)[None]


def solution(mesh):
    in_specs = (
        P("section", "expert", None),
        P("section", None),
        P("section", "expert", None, None),
        P("section", "expert", None, None),
        P("section", "expert", None, None),
        P(None, "section", "expert", None),
        P(None, "section", "expert", None),
    )
    return jax.shard_map(
        on_device, mesh=mesh, in_specs=in_specs, out_specs=P("section", "expert", None), check_vma=False
    )
```

time: 261 us -> 241 us (0.923)
  waiting for transfers between devices: 64.9 us -> 32.9 us
  blocking collectives: 135 us -> 150 us
  starting transfers between devices: 10.1 us -> 5.27 us
  Pallas kernels: 45.3 us -> 49.1 us
    all_to_all x1 -> x0, waiting for transfers between devices: 44.5 us -> none  [exchange(): lax.all_to_all(blocks.reshape(experts, capacity, width), 'expert', 0, 0,...]
    all_to_all x3 -> x4, blocking collectives: 135 us -> 150 us  [exchange(): lax.all_to_all(blocks.reshape(experts, capacity, width), 'expert', 0, 0,...]
    ppermute x4, waiting for transfers between devices: 20.4 us -> 32.9 us  [moved_from(): return lax.ppermute(value, ('section', 'expert'), pairs)]
    all_to_all x1 -> x0, starting transfers between devices: 4.85 us -> none  [exchange(): lax.all_to_all(blocks.reshape(experts, capacity, width), 'expert', 0, 0,...]
    pallas_call x6, Pallas kernels: 45.3 us -> 49.1 us  [the longest x2 35.2 us: mlp(): pl.pallas_call(functools.partial(mlp_kernel, widths, turn, depth, in_tile...]
  transfers between devices with their start and end apart: 5 -> 4, of which waited for: 4 -> 3; matrix products, arithmetic and copies ran while one was open for 0% -> 0% of each run, Pallas kernels for 8% -> 10%
where the time goes in v3:
time: 241 us; the launch traced here: 240 us
  blocking collectives  150 us (62%)
  Pallas kernels  49.1 us (20%)
  waiting for transfers between devices  32.9 us (14%)
  starting transfers between devices  5.27 us (2%)
    all_to_all x4, blocking collectives, exchange(): lax.all_to_all(blocks.reshape(experts, capacity, width), 'expert', 0, 0,...  150 us
    pallas_call x2, Pallas kernels, mlp(): pl.pallas_call(functools.partial(mlp_kernel, widths, turn, depth, in_tile...  35.2 us
    ppermute x4, waiting for transfers between devices, moved_from(): return lax.ppermute(value, ('section', 'expert'), pairs)  32.9 us
    pallas_call x2, Pallas kernels, pack(): pl.pallas_call(functools.partial(pack_kernel, step, experts, capacity, ti...  7.02 us
    pallas_call x2, Pallas kernels, combine(): pl.pallas_call(functools.partial(combine_kernel, step, experts, capacity,...  6.88 us
    ppermute x4, starting transfers between devices, moved_from(): return lax.ppermute(value, ('section', 'expert'), pairs)  5.27 us
  transfers between devices with their start and end apart: 4, of which 3 were waited for; matrix products, arithmetic and copies ran while one was open for 0% of the time, Pallas kernels for 10%

profile of v3, /device:TPU:0, one launch (start us, length us, event | category | flops | bytes accessed | tf_op | source)
XLA Modules:
  0.0 240.5 jit_solution(11399583713860337516)
XLA Ops:
  0.0 3.9 %pack.5 = (bf16[512,3584]{1,0:T(8,128)(2,1)S(1)}, bf16[512,512]{1,0:T(8,128)(2,1)S(1)}, bf16[512,3072]{1,0:T(8,128)(2,1)}) custom-call(s32[1]{0:T(128)} %bitcast.30.refs_0_, bf16[128,3584]{1,0:T(8,128)(2,1)} %bitcast.46, f32[1,3584]{1,0:T(1,128)} %refs_2_.1, s32[2,2,128]{2,1,0:T(2,128)} %bitcast.61), custom_call_target="tpu_custom_call" | custom-call | flops 469762048 | bytes 4587520 | tf_op jit(solution)/shard_map/pack/pallas_call | solution.py:75
  3.9 99.1 %conditional.5 = (bf16[128,3584]{1,0:T(8,128)(2,1)}) conditional(s32[]{:T(128)} %convert_element_type.2, (bf16[512,3584]{1,0:T(8,128)(2,1)S(1)}, bf16[1,1,3584,1024]{3,2,1,0:T(8,128)(2,1)}, bf16[1,1,3584,1024]{3,2,1,0:T(8,128)(2,1)}, bf16[1,1,1024,3584]{3,2,1,0:T(8,128)(2,1)}, bf16[128,3584]{1,0:T(8,128)(2,1)}, /*index=5*/s32[2,2,128]{2,1,0:T(2,128)}, ...), branch_computations={%region_0.1_spmd, %region_1.2_spmd} | conditional | flops 12213813248 | bytes 53231708 | solution.py:321
  3.9 39.8 %all_to_all.36 = bf16[32,16,3584]{2,1,0:T(8,128)(2,1)} all-to-all(bf16[32,16,3584]{2,1,0:T(8,128)(2,1)S(1)} %bitcast.49), channel_id=1, replica_groups=mesh['section'=4,'expert'=32] {'expert'}, dimensions={0} | all-to-all | bytes 7340032 | tf_op jit(solution)/shard_map/cond/branch_0_fun/all_to_all | solution.py:279
  43.7 17.6 %mlp.4 = bf16[512,3584]{1,0:T(8,128)(2,1)} custom-call(bf16[512,3584]{1,0:T(8,128)(2,1)} %bitcast.56, bf16[3584,1024]{1,0:T(8,128)(2,1)} %bitcast.70, bf16[3584,1024]{1,0:T(8,128)(2,1)} %bitcast.74, bf16[1024,3584]{1,0:T(8,128)(2,1)} %bitcast.78), custom_call_target="tpu_custom_call" | custom-call | flops 11274289152 | bytes 29360128 | tf_op jit(solution)/shard_map/cond/branch_0_fun/mlp/pallas_call | solution.py:193
  61.4 37.9 %all_to_all.37 = bf16[32,16,3584]{2,1,0:T(8,128)(2,1)} all-to-all(bf16[32,16,3584]{2,1,0:T(8,128)(2,1)} %bitcast.51), channel_id=1, replica_groups=mesh['section'=4,'expert'=32] {'expert'}, dimensions={0} | all-to-all | bytes 7340032 | tf_op jit(solution)/shard_map/cond/branch_0_fun/all_to_all | solution.py:279
  99.3 3.7 %combine.4 = bf16[128,3584]{1,0:T(8,128)(2,1)} custom-call(bf16[512,3584]{1,0:T(8,128)(2,1)} %bitcast.40, bf16[128,3584]{1,0:T(8,128)(2,1)S(1)} %copy-done, s32[2,2,128]{2,1,0:T(2,128)S(1)} %copy-done.2, f32[2,2,128]{2,1,0:T(2,128)S(1)} %copy-done.7), custom_call_target="tpu_custom_call" | custom-call | flops 939524096 | bytes 5505024 | tf_op jit(solution)/shard_map/cond/branch_0_fun/combine/pallas_call | solution.py:258
  103.1 1.3 collective-permute-start
  104.4 0.3 conditional.8
  104.5 0.1 broadcast.14
  104.7 1.3 collective-permute-start.2
  106.0 0.7 collective-permute-done
  106.7 1.0 conditional.6
  106.7 1.0 broadcast.12
  107.6 1.3 collective-permute-start.1
  108.9 23.4 %collective-permute-done.2 = bf16[128,3584]{1,0:T(8,128)(2,1)S(1)} collective-permute-done((bf16[128,3584]{1,0:T(8,128)(2,1)S(1)}, bf16[128,3584]{1,0:T(8,128)(2,1)S(1)}, u32[]{:S(2)}, u32[]{:S(2)}) %collective-permute-start.2) | collective-permute-done | bytes 917536 | tf_op jit(solution)/shard_map/ppermute | solution.py:290
  132.3 95.7 %conditional.9 = (bf16[128,3584]{1,0:T(8,128)(2,1)S(1)}) conditional(s32[]{:T(128)} %convert_element_type.2, (bf16[128,3584]{1,0:T(8,128)(2,1)S(1)}, f32[1,3584]{1,0:T(1,128)S(1)}, s32[2,2,128]{2,1,0:T(2,128)}, bf16[1,1,3584,1024]{3,2,1,0:T(8,128)(2,1)}, bf16[1,1,3584,1024]{3,2,1,0:T(8,128)(2,1)}, /*index=5*/bf16[1,1,1024,3584]{3,2,1,0:T(8,128)(2,1)}, ...), branch_computations={%region_8.9_spmd, %region_9.10_spmd} | conditional | flops 12683575296 | bytes 54149184 | solution.py:327
  132.3 3.1 %pack.4 = bf16[512,3584]{1,0:T(8,128)(2,1)} custom-call(bf16[128,3584]{1,0:T(8,128)(2,1)S(1)} %get-tuple-element.108.refs_0_.x_hbm, f32[1,3584]{1,0:T(1,128)S(1)} %get-tuple-element.109.refs_1_, s32[2,2,128]{2,1,0:T(2,128)} %get-tuple-element.110.refs_2_.routes_ref), custom_call_target="tpu_custom_call" | custom-call | flops 469762048 | bytes 4587520 | tf_op jit(solution)/shard_map/cond/branch_0_fun/pack/pallas_call | solution.py:75
  135.4 36.1 %all_to_all.43 = bf16[32,16,3584]{2,1,0:T(8,128)(2,1)} all-to-all(bf16[32,16,3584]{2,1,0:T(8,128)(2,1)} %bitcast.45), channel_id=1, replica_groups=mesh['section'=4,'expert'=32] {'expert'}, dimensions={0} | all-to-all | bytes 7340032 | tf_op jit(solution)/shard_map/cond/branch_0_fun/all_to_all | solution.py:279
  171.5 17.6 %mlp.7 = bf16[512,3584]{1,0:T(8,128)(2,1)} custom-call(bf16[512,3584]{1,0:T(8,128)(2,1)} %bitcast.54, bf16[3584,1024]{1,0:T(8,128)(2,1)} %bitcast.73, bf16[3584,1024]{1,0:T(8,128)(2,1)} %bitcast.77, bf16[1024,3584]{1,0:T(8,128)(2,1)} %bitcast.81, bf16[128,3584]{1,0:T(8,128)(2,1)} %get-tuple-element.114.refs_4_), custom_call_target="tpu_custom_call" | custom-call | flops 11274289152 | bytes 29360128 | tf_op jit(solution)/shard_map/cond/branch_0_fun/mlp/pallas_call | solution.py:193
  189.1 35.8 %all_to_all.44 = bf16[32,16,3584]{2,1,0:T(8,128)(2,1)} all-to-all(bf16[32,16,3584]{2,1,0:T(8,128)(2,1)} %bitcast.55), channel_id=1, replica_groups=mesh['section'=4,'expert'=32] {'expert'}, dimensions={0} | all-to-all | bytes 7340032 | tf_op jit(solution)/shard_map/cond/branch_0_fun/all_to_all | solution.py:279
  224.9 3.1 %combine.7 = bf16[128,3584]{1,0:T(8,128)(2,1)S(1)} custom-call(bf16[512,3584]{1,0:T(8,128)(2,1)} %bitcast.43, bf16[128,3584]{1,0:T(8,128)(2,1)S(1)} %get-tuple-element.108.refs_0_.x_hbm, s32[2,2,128]{2,1,0:T(2,128)S(1)} %copy-done.5, f32[2,2,128]{2,1,0:T(2,128)S(1)} %copy-done.10), custom_call_target="tpu_custom_call" | custom-call | flops 939524096 | bytes 5505024 | tf_op jit(solution)/shard_map/cond/branch_0_fun/combine/pallas_call | solution.py:258
  228.0 1.3 collective-permute-start.3
  229.4 8.9 %collective-permute-done.1 = bf16[128,3584]{1,0:T(8,128)(2,1)} collective-permute-done((bf16[128,3584]{1,0:T(8,128)(2,1)}, bf16[128,3584]{1,0:T(8,128)(2,1)}, u32[]{:S(2)}, u32[]{:S(2)}) %collective-permute-start.1) | collective-permute-done | bytes 917536 | tf_op jit(solution)/shard_map/ppermute | solution.py:290
  238.3 2.2 select_bitcast_fusion
  (14 shorter events, 0.0 us)
Async XLA Ops:
  61.3 38.0 %copy-start = (bf16[128,3584]{1,0:T(8,128)(2,1)S(1)}, bf16[128,3584]{1,0:T(8,128)(2,1)}, u32[]{:S(2)}) copy-start(bf16[128,3584]{1,0:T(8,128)(2,1)} %get-tuple-element.87.x_hbm) | copy-start | bytes 2752516 | tf_op jit(solution)/shard_map/cond
  61.3 38.0 %copy-start.2 = (s32[2,2,128]{2,1,0:T(2,128)S(1)}, s32[2,2,128]{2,1,0:T(2,128)}, u32[]{:S(2)}) copy-start(s32[2,2,128]{2,1,0:T(2,128)} %get-tuple-element.88.routes_ref) | copy-start | bytes 6148 | tf_op jit(solution)/shard_map/cond
  61.4 38.0 %copy-start.7 = (f32[2,2,128]{2,1,0:T(2,128)S(1)}, f32[2,2,128]{2,1,0:T(2,128)}, u32[]{:S(2)}) copy-start(f32[2,2,128]{2,1,0:T(2,128)} %get-tuple-element.89.logits_ref) | copy-start | bytes 6148 | tf_op jit(solution)/shard_map/cond
  103.1 3.6 %collective-permute-start = (bf16[128,3584]{1,0:T(8,128)(2,1)}, bf16[128,3584]{1,0:T(8,128)(2,1)S(1)}, u32[]{:S(2)}, u32[]{:S(2)}) collective-permute-start(bf16[128,3584]{1,0:T(8,128)(2,1)} %get-tuple-element.122), channel_id=1, source_target_pairs={{0,32},{1,33},{2,34},{3,35},{4,36},{5,37},{6,38},{7,39},{8,40},{9,... | collective-permute-start | bytes 2752520 | tf_op jit(solution)/shard_map/ppermute | solution.py:290
  104.4 2.2 copy-start.6
  104.7 27.6 %collective-permute-start.2 = (bf16[128,3584]{1,0:T(8,128)(2,1)S(1)}, bf16[128,3584]{1,0:T(8,128)(2,1)S(1)}, u32[]{:S(2)}, u32[]{:S(2)}) collective-permute-start(bf16[128,3584]{1,0:T(8,128)(2,1)S(1)} %get-tuple-element.125), channel_id=1, source_target_pairs={{32,64},{33,65},{34,66},{35,67},{36,68},{37,69},{38,70},{39,71},{4... | collective-permute-start | bytes 2752520 | tf_op jit(solution)/shard_map/ppermute | solution.py:290
  107.6 130.6 %collective-permute-start.1 = (bf16[128,3584]{1,0:T(8,128)(2,1)}, bf16[128,3584]{1,0:T(8,128)(2,1)}, u32[]{:S(2)}, u32[]{:S(2)}) collective-permute-start(bf16[128,3584]{1,0:T(8,128)(2,1)} %get-tuple-element.123), channel_id=1, source_target_pairs={{32,64},{33,65},{34,66},{35,67},{36,68},{37,69},{38,70},{39,71},{4... | collective-permute-start | bytes 2752520 | tf_op jit(solution)/shard_map/ppermute | solution.py:290
  189.1 35.8 %copy-start.5 = (s32[2,2,128]{2,1,0:T(2,128)S(1)}, s32[2,2,128]{2,1,0:T(2,128)}, u32[]{:S(2)}) copy-start(s32[2,2,128]{2,1,0:T(2,128)} %get-tuple-element.110.refs_2_.routes_ref) | copy-start | bytes 6148 | tf_op jit(solution)/shard_map/cond
  189.1 35.8 %copy-start.10 = (f32[2,2,128]{2,1,0:T(2,128)S(1)}, f32[2,2,128]{2,1,0:T(2,128)}, u32[]{:S(2)}) copy-start(f32[2,2,128]{2,1,0:T(2,128)} %get-tuple-element.115.logits_ref) | copy-start | bytes 6148 | tf_op jit(solution)/shard_map/cond
  228.0 10.2 %collective-permute-start.3 = (bf16[128,3584]{1,0:T(8,128)(2,1)S(1)}, bf16[128,3584]{1,0:T(8,128)(2,1)S(1)}, u32[]{:S(2)}, u32[]{:S(2)}) collective-permute-start(bf16[128,3584]{1,0:T(8,128)(2,1)S(1)} %get-tuple-element.126), channel_id=1, source_target_pairs={{0,32},{1,33},{2,34},{3,35},{4,36},{5,37},{6,38},{7,39},{8,40},{9,... | collective-permute-start | bytes 2752520 | tf_op jit(solution)/shard_map/ppermute | solution.py:290

commit v4 on v3

--- a/solution.py
+++ b/solution.py
@@ -10,8 +10,9 @@
 TOP = 2
 STEPS = 2
 EPSILON = 1e-06
-VMEM_LIMIT = 56 * 1024 * 1024
-PARAMS = pltpu.CompilerParams(vmem_limit_bytes=VMEM_LIMIT)
+MIB = 1024 * 1024
+PARAMS = pltpu.CompilerParams(vmem_limit_bytes=16 * MIB)
+MLP_PARAMS = pltpu.CompilerParams(vmem_limit_bytes=36 * MIB)
 ANY = pl.BlockSpec(memory_space=pl.ANY)
 VMEM = pl.BlockSpec(memory_space=pltpu.VMEM)
 
@@ -33,12 +34,10 @@
     return [(start, min(size, total - start)) for start in range(0, total, size)]
 
 
-def pack_kernel(step, experts, capacity, tile, widths, *refs):
-    if widths:
-        flag_ref, x_ref, gain_ref, routes_ref, whole_hbm, *parts, held_ref, sems = refs
-    else:
-        x_ref, gain_ref, routes_ref, whole_hbm, held_ref, sems = refs
-        parts = []
+def pack_kernel(step, experts, capacity, tile, kinds, *refs):
+    if len(kinds) > 1:
+        flag_ref, *refs = refs
+    x_ref, gain_ref, routes_ref, *outs, held_ref, sems = refs
     rows, width = x_ref.shape
     slots = experts * capacity
     keys = slot_rows(routes_ref[step], experts, capacity)
@@ -46,17 +45,18 @@
     pick = jnp.where((keys[0] == lines) | (keys[1] == lines), 1.0, 0.0).astype(jnp.bfloat16)
     values = x_ref[...].astype(jnp.float32)
     scale = lax.rsqrt(jnp.mean(values * values, axis=-1, keepdims=True) + EPSILON)
-    targets = [part.at[:, start : start + tile] for part, size in zip(parts, widths) for start in range(0, size, tile)]
+    targets = []
+    for widths in kinds:
+        parts, outs = outs[: len(widths)], outs[len(widths) :]
+        targets.append([part.at[:, start : start + tile] for part, size in zip(parts, widths) for start in range(0, size, tile)])
 
     def each(i, start, size, act):
-        source = held_ref.at[:, start : start + size]
-        whole = pltpu.make_async_copy(source, whole_hbm.at[:, start : start + size], sems.at[i])
-        if targets:
-            part = pltpu.make_async_copy(source, targets[i], sems.at[i])
-            pl.when(flag_ref[0] == 0)(lambda: act(whole))
-            pl.when(flag_ref[0] == 1)(lambda: act(part))
+        copies = [pltpu.make_async_copy(held_ref.at[:, start : start + size], places[i], sems.at[i]) for places in targets]
+        if len(copies) == 1:
+            act(copies[0])
         else:
-            act(whole)
+            for value, copy in enumerate(copies):
+                pl.when(flag_ref[0] == value)(functools.partial(act, copy))
 
     for i, (start, size) in enumerate(cuts(width, tile)):
         values = x_ref[:, start : start + size].astype(jnp.float32)
@@ -67,13 +67,13 @@
         each(i, start, size, lambda copy: copy.wait())
 
 
-def pack(step, x, gain, routes, experts, capacity, flag=None, widths=(), tile=512):
+def pack(step, x, gain, routes, experts, capacity, *kinds, flag=None, tile=512):
     rows, width = x.shape
     slots = experts * capacity
-    shapes = [jax.ShapeDtypeStruct((slots, size), jnp.bfloat16) for size in (width, *widths)]
-    flags = [flag] if widths else []
-    out = pl.pallas_call(
-        functools.partial(pack_kernel, step, experts, capacity, tile, widths),
+    shapes = [jax.ShapeDtypeStruct((slots, size), jnp.bfloat16) for widths in kinds for size in widths]
+    flags = [flag] if len(kinds) > 1 else []
+    return pl.pallas_call(
+        functools.partial(pack_kernel, step, experts, capacity, tile, kinds),
         in_specs=[pl.BlockSpec(memory_space=pltpu.SMEM)] * len(flags) + [VMEM, VMEM, VMEM],
         out_specs=[ANY] * len(shapes),
         out_shape=shapes,
@@ -82,7 +82,6 @@
         cost_estimate=pl.CostEstimate(flops=2 * rows * slots * width, bytes_accessed=2 * (rows + slots) * width, transcendentals=0),
         name="pack",
     )(*flags, x, gain, routes)
-    return out if widths else out[0]
 
 
 def mlp_kernel(widths, turn, depth, in_tile, down_tile, *refs):
@@ -208,7 +207,7 @@
             dma((downs,)),
             dma((2, downs)),
         ],
-        compiler_params=PARAMS,
+        compiler_params=MLP_PARAMS,
         cost_estimate=pl.CostEstimate(
             flops=6 * slots * width * inner,
             bytes_accessed=2 * (2 * slots * width + 3 * width * inner),
@@ -252,7 +251,7 @@
         copy.wait()
 
 
-def combine(step, back, x, routes, logits, experts, capacity, tile=896):
+def combine(step, back, x, routes, logits, experts, capacity, tile=1024):
     slots, width = back.shape
     rows = x.shape[0]
     return pl.pallas_call(
@@ -271,7 +270,8 @@
         cost_estimate=pl.CostEstimate(flops=4 * rows * slots * width, bytes_accessed=2 * (2 * rows + slots) * width, transcendentals=0),
         name="combine",
     )(back, x, routes, logits)
-PARTS = (512, 3072)
+FIRST_PARTS = (512, 3072)
+LAST_PARTS = (3584,)
 
 
 def exchange(blocks, experts, capacity):
@@ -280,37 +280,22 @@
     return moved.reshape(experts * capacity, width)
 
 
-def moved_from(value, odd, turn=0):
-    sections, experts = lax.axis_size("section"), lax.axis_size("expert")
-    pairs = [
-        (i * experts + j, (i + 1) % sections * experts + (j + turn) % experts)
-        for i in range(odd, sections, 2)
-        for j in range(experts)
-    ]
-    return lax.ppermute(value, ("section", "expert"), pairs)
+def moved_from(value, odd):
+    sections = lax.axis_size("section")
+    return lax.ppermute(value, "section", [(i, (i + 1) % sections) for i in range(odd, sections, 2)])
 
 
 def on_device(activations, norm_gain, w_gate, w_up, w_down, routes, gate_logits):
     experts = lax.axis_size("expert")
-    capacity = 2 * activations.shape[1] * TOP // experts
+    start = activations[0]
+    capacity = 2 * start.shape[0] * TOP // experts
     chosen, logits = (value[:, 0].transpose(0, 2, 1) for value in (routes, gate_logits))
-    start = activations[0]
     parity = lax.axis_index("section") % 2
     odd = parity == 1
     nothing = functools.partial(jnp.zeros_like, start)
-
-    def spread(step, current):
-        return exchange(pack(step, current, norm_gain, chosen, experts, capacity), experts, capacity)
-
-    def gather(step, current, rows, *after):
-        produced = mlp(rows, w_gate[0, 0], w_up[0, 0], w_down[0, 0], *after)
-        back = exchange(produced, experts, capacity)
-        return combine(step, back, current, chosen, logits, experts, capacity)
-
-    flag = parity.astype(jnp.int32).reshape(1)
-    whole, *parts = pack(0, start, norm_gain, chosen, experts, capacity, flag, PARTS)
-
-    def in_turn():
+    whole = (start.shape[1],)
+
+    def in_turn(parts):
         rows = []
         for part in parts:
             if rows:
@@ -318,13 +303,23 @@
             rows.append(exchange(part, experts, capacity))
         return rows
 
-    first_even = lax.cond(odd, nothing, lambda: gather(0, start, (exchange(whole, experts, capacity),)))
+    def layer(step, current, packed, *after):
+        produced = mlp(in_turn(packed), w_gate[0, 0], w_up[0, 0], w_down[0, 0], *after)
+        back = exchange(produced, experts, capacity)
+        return combine(step, back, current, chosen, logits, experts, capacity)
+
+    def packed_rows(step, current, *kinds, flag=None):
+        return pack(step, current, norm_gain, chosen, experts, capacity, *kinds, flag=flag)
+
+    flag = parity.astype(jnp.int32).reshape(1)
+    packed = packed_rows(0, start, whole, FIRST_PARTS, flag=flag)
+    first_even = lax.cond(odd, nothing, lambda: layer(0, start, packed[:1]))
     near = moved_from(first_even, 0)
-    first_odd = lax.cond(odd, lambda: gather(0, start, in_turn(), first_even), nothing)
+    first_odd = lax.cond(odd, lambda: layer(0, start, packed[1:], first_even), nothing)
     far = moved_from(first_odd, 1)
-    early = lax.cond(odd, lambda: gather(1, near, (spread(1, near),)), nothing)
+    early = lax.cond(odd, lambda: layer(1, near, packed_rows(1, near, whole)), nothing)
     far_out = moved_from(early, 1)
-    late = lax.cond(odd, nothing, lambda: gather(1, far, (spread(1, far),), early))
+    late = lax.cond(odd, nothing, lambda: layer(1, far, packed_rows(1, far, LAST_PARTS), early))
     near_out = moved_from(late, 0)
     kept = lax.cond(odd, nothing, lambda: far_out + jnp.bfloat16(0))
     return jnp.where(parity == 0, kept, near_out)[None]

time: 241 us -> 233 us (0.967)
  blocking collectives: 150 us -> 141 us
  waiting for transfers between devices: 32.9 us -> 36 us
  Pallas kernels: 49.1 us -> 46.3 us
    all_to_all x4, blocking collectives: 150 us -> 141 us  [exchange(): lax.all_to_all(blocks.reshape(experts, capacity, width), 'expert', 0, 0,...]
    ppermute x4, waiting for transfers between devices: 32.9 us -> 36 us  [moved_from(): lax.ppermute(value, 'section', [(i, (i + 1) % sections) for i in range(od...]
where the time goes in v4:
time: 233 us
  blocking collectives  141 us (61%)
  Pallas kernels  46.3 us (20%)
  waiting for transfers between devices  36 us (15%)
  starting transfers between devices  5.27 us (2%)
    all_to_all x4, blocking collectives, exchange(): lax.all_to_all(blocks.reshape(experts, capacity, width), 'expert', 0, 0,...  141 us
    ppermute x4, waiting for transfers between devices, moved_from(): lax.ppermute(value, 'section', [(i, (i + 1) % sections) for i in range(od...  36 us
    pallas_call x2, Pallas kernels, mlp(): pl.pallas_call(functools.partial(mlp_kernel, widths, turn, depth, in_tile...  33.4 us
    pallas_call x2, Pallas kernels, pack(): pl.pallas_call(functools.partial(pack_kernel, step, experts, capacity, ti...  7.23 us
    pallas_call x2, Pallas kernels, combine(): pl.pallas_call(functools.partial(combine_kernel, step, experts, capacity,...  5.69 us
    ppermute x4, starting transfers between devices, moved_from(): lax.ppermute(value, 'section', [(i, (i + 1) % sections) for i in range(od...  5.27 us
  transfers between devices with their start and end apart: 4, of which 3 were waited for; matrix products, arithmetic and copies ran while one was open for 0% of the time, Pallas kernels for 10%

profile of v4, /device:TPU:0, one launch (start us, length us, event | category | flops | bytes accessed | tf_op | source)
XLA Modules:
  0.0 232.8 jit_solution(10140459999777390823)
XLA Ops:
  0.0 3.9 %pack.5 = (bf16[512,3584]{1,0:T(8,128)(2,1)S(1)}, bf16[512,512]{1,0:T(8,128)(2,1)S(1)}, bf16[512,3072]{1,0:T(8,128)(2,1)}) custom-call(s32[1]{0:T(128)} %bitcast.30.refs_0_, bf16[128,3584]{1,0:T(8,128)(2,1)} %bitcast.55, f32[1,3584]{1,0:T(1,128)} %refs_2_.1, s32[2,2,128]{2,1,0:T(2,128)} %bitcast.61), custom_call_target="tpu_custom_call" | custom-call | flops 469762048 | bytes 4587520 | tf_op jit(solution)/shard_map/pack/pallas_call | solution.py:75
  3.9 98.9 %conditional.5 = (bf16[128,3584]{1,0:T(8,128)(2,1)}) conditional(s32[]{:T(128)} %convert_element_type.2, (bf16[512,3584]{1,0:T(8,128)(2,1)S(1)}, bf16[1,1,3584,1024]{3,2,1,0:T(8,128)(2,1)}, bf16[1,1,3584,1024]{3,2,1,0:T(8,128)(2,1)}, bf16[1,1,1024,3584]{3,2,1,0:T(8,128)(2,1)}, bf16[128,3584]{1,0:T(8,128)(2,1)}, /*index=5*/s32[2,2,128]{2,1,0:T(2,128)}, ...), branch_computations={%region_0.1_spmd, %region_1.2_spmd} | conditional | flops 12213813248 | bytes 82591872 | solution.py:316
  3.9 40.2 %all_to_all.36 = bf16[32,16,3584]{2,1,0:T(8,128)(2,1)S(1)} all-to-all(bf16[32,16,3584]{2,1,0:T(8,128)(2,1)S(1)} %bitcast.58), channel_id=1, replica_groups=mesh['section'=4,'expert'=32] {'expert'}, dimensions={0} | all-to-all | bytes 7340032 | tf_op jit(solution)/shard_map/cond/branch_0_fun/all_to_all | solution.py:279
  44.2 16.7 %mlp.4 = bf16[512,3584]{1,0:T(8,128)(2,1)S(1)} custom-call(bf16[512,3584]{1,0:T(8,128)(2,1)S(1)} %bitcast.52, bf16[3584,1024]{1,0:T(8,128)(2,1)S(1)} %bitcast.70, bf16[3584,1024]{1,0:T(8,128)(2,1)} %bitcast.74, bf16[1024,3584]{1,0:T(8,128)(2,1)} %bitcast.78), custom_call_target="tpu_custom_call" | custom-call | flops 11274289152 | bytes 29360128 | tf_op jit(solution)/shard_map/cond/branch_0_fun/mlp/pallas_call | solution.py:192
  60.9 38.7 %all_to_all.37 = bf16[32,16,3584]{2,1,0:T(8,128)(2,1)S(1)} all-to-all(bf16[32,16,3584]{2,1,0:T(8,128)(2,1)S(1)} %bitcast.47), channel_id=1, replica_groups=mesh['section'=4,'expert'=32] {'expert'}, dimensions={0} | all-to-all | bytes 7340032 | tf_op jit(solution)/shard_map/cond/branch_0_fun/all_to_all | solution.py:279
  99.6 3.1 %combine.4 = bf16[128,3584]{1,0:T(8,128)(2,1)} custom-call(bf16[512,3584]{1,0:T(8,128)(2,1)S(1)} %bitcast.40, bf16[128,3584]{1,0:T(8,128)(2,1)S(1)} %copy-done, s32[2,2,128]{2,1,0:T(2,128)S(1)} %copy-done.2, f32[2,2,128]{2,1,0:T(2,128)S(1)} %copy-done.7), custom_call_target="tpu_custom_call" | custom-call | flops 939524096 | bytes 5505024 | tf_op jit(solution)/shard_map/cond/branch_0_fun/combine/pallas_call | solution.py:257
  102.8 1.3 collective-permute-start
  104.1 0.3 conditional.8
  104.2 0.1 broadcast.14
  104.5 1.3 collective-permute-start.2
  105.8 0.6 collective-permute-done
  106.4 1.0 conditional.6
  106.4 1.0 broadcast.12
  107.4 1.3 collective-permute-start.1
  108.6 26.8 %collective-permute-done.2 = bf16[128,3584]{1,0:T(8,128)(2,1)S(1)} collective-permute-done((bf16[128,3584]{1,0:T(8,128)(2,1)S(1)}, bf16[128,3584]{1,0:T(8,128)(2,1)S(1)}, u32[]{:S(2)}, u32[]{:S(2)}) %collective-permute-start.2) | collective-permute-done | bytes 917536 | tf_op jit(solution)/shard_map/ppermute | solution.py:285
  135.5 85.2 %conditional.9 = (bf16[128,3584]{1,0:T(8,128)(2,1)S(1)}) conditional(s32[]{:T(128)} %convert_element_type.2, (bf16[128,3584]{1,0:T(8,128)(2,1)S(1)}, f32[1,3584]{1,0:T(1,128)S(1)}, s32[2,2,128]{2,1,0:T(2,128)}, bf16[1,1,3584,1024]{3,2,1,0:T(8,128)(2,1)}, bf16[1,1,3584,1024]{3,2,1,0:T(8,128)(2,1)}, /*index=5*/bf16[1,1,1024,3584]{3,2,1,0:T(8,128)(2,1)}, ...), branch_computations={%region_8.9_spmd, %region_9.10_spmd} | conditional | flops 12683575296 | bytes 83509344 | solution.py:322
  135.5 3.3 %pack.4 = bf16[512,3584]{1,0:T(8,128)(2,1)S(1)} custom-call(bf16[128,3584]{1,0:T(8,128)(2,1)S(1)} %get-tuple-element.108.refs_0_.x_hbm, f32[1,3584]{1,0:T(1,128)S(1)} %get-tuple-element.109.refs_1_, s32[2,2,128]{2,1,0:T(2,128)} %get-tuple-element.110.refs_2_.routes_ref), custom_call_target="tpu_custom_call" | custom-call | flops 469762048 | bytes 4587520 | tf_op jit(solution)/shard_map/cond/branch_0_fun/pack/pallas_call | solution.py:75
  138.8 31.3 %all_to_all.43 = bf16[32,16,3584]{2,1,0:T(8,128)(2,1)S(1)} all-to-all(bf16[32,16,3584]{2,1,0:T(8,128)(2,1)S(1)} %bitcast.45), channel_id=1, replica_groups=mesh['section'=4,'expert'=32] {'expert'}, dimensions={0} | all-to-all | bytes 7340032 | tf_op jit(solution)/shard_map/cond/branch_0_fun/all_to_all | solution.py:279
  170.1 16.7 %mlp.7 = bf16[512,3584]{1,0:T(8,128)(2,1)S(1)} custom-call(bf16[512,3584]{1,0:T(8,128)(2,1)S(1)} %bitcast.50, bf16[3584,1024]{1,0:T(8,128)(2,1)S(1)} %bitcast.73, bf16[3584,1024]{1,0:T(8,128)(2,1)} %bitcast.77, bf16[1024,3584]{1,0:T(8,128)(2,1)} %bitcast.81, bf16[128,3584]{1,0:T(8,128)(2,1)} %get-tuple-element.114.refs_4_), custom_call_target="tpu_custom_call" | custom-call | flops 11274289152 | bytes 29360128 | tf_op jit(solution)/shard_map/cond/branch_0_fun/mlp/pallas_call | solution.py:192
  186.8 31.0 %all_to_all.44 = bf16[32,16,3584]{2,1,0:T(8,128)(2,1)S(1)} all-to-all(bf16[32,16,3584]{2,1,0:T(8,128)(2,1)S(1)} %bitcast.51), channel_id=1, replica_groups=mesh['section'=4,'expert'=32] {'expert'}, dimensions={0} | all-to-all | bytes 7340032 | tf_op jit(solution)/shard_map/cond/branch_0_fun/all_to_all | solution.py:279
  217.8 2.5 %combine.7 = bf16[128,3584]{1,0:T(8,128)(2,1)S(1)} custom-call(bf16[512,3584]{1,0:T(8,128)(2,1)S(1)} %bitcast.43, bf16[128,3584]{1,0:T(8,128)(2,1)S(1)} %get-tuple-element.108.refs_0_.x_hbm, s32[2,2,128]{2,1,0:T(2,128)S(1)} %copy-done.5, f32[2,2,128]{2,1,0:T(2,128)S(1)} %copy-done.10), custom_call_target="tpu_custom_call" | custom-call | flops 939524096 | bytes 5505024 | tf_op jit(solution)/shard_map/cond/branch_0_fun/combine/pallas_call | solution.py:257
  220.7 1.3 collective-permute-start.3
  222.0 8.6 %collective-permute-done.1 = bf16[128,3584]{1,0:T(8,128)(2,1)} collective-permute-done((bf16[128,3584]{1,0:T(8,128)(2,1)}, bf16[128,3584]{1,0:T(8,128)(2,1)}, u32[]{:S(2)}, u32[]{:S(2)}) %collective-permute-start.1) | collective-permute-done | bytes 917536 | tf_op jit(solution)/shard_map/ppermute | solution.py:285
  230.6 2.2 select_bitcast_fusion
  (18 shorter events, 0.1 us)
Async XLA Ops:
  3.9 40.2 %copy-start.11 = (bf16[1,1,3584,1024]{3,2,1,0:T(8,128)(2,1)S(1)}, bf16[1,1,3584,1024]{3,2,1,0:T(8,128)(2,1)}, u32[]{:S(2)}) copy-start(bf16[1,1,3584,1024]{3,2,1,0:T(8,128)(2,1)} %get-tuple-element.82) | copy-start | bytes 22020100 | tf_op jit(solution)/shard_map/cond
  60.9 38.7 %copy-start = (bf16[128,3584]{1,0:T(8,128)(2,1)S(1)}, bf16[128,3584]{1,0:T(8,128)(2,1)}, u32[]{:S(2)}) copy-start(bf16[128,3584]{1,0:T(8,128)(2,1)} %get-tuple-element.87.x_hbm) | copy-start | bytes 2752516 | tf_op jit(solution)/shard_map/cond
  60.9 38.7 %copy-start.2 = (s32[2,2,128]{2,1,0:T(2,128)S(1)}, s32[2,2,128]{2,1,0:T(2,128)}, u32[]{:S(2)}) copy-start(s32[2,2,128]{2,1,0:T(2,128)} %get-tuple-element.88.routes_ref) | copy-start | bytes 6148 | tf_op jit(solution)/shard_map/cond
  60.9 38.7 %copy-start.7 = (f32[2,2,128]{2,1,0:T(2,128)S(1)}, f32[2,2,128]{2,1,0:T(2,128)}, u32[]{:S(2)}) copy-start(f32[2,2,128]{2,1,0:T(2,128)} %get-tuple-element.89.logits_ref) | copy-start | bytes 6148 | tf_op jit(solution)/shard_map/cond
  102.8 3.6 %collective-permute-start = (bf16[128,3584]{1,0:T(8,128)(2,1)}, bf16[128,3584]{1,0:T(8,128)(2,1)S(1)}, u32[]{:S(2)}, u32[]{:S(2)}) collective-permute-start(bf16[128,3584]{1,0:T(8,128)(2,1)} %get-tuple-element.122), channel_id=1, source_target_pairs={{0,32},{64,96},{1,33},{65,97},{2,34},{66,98},{3,35},{67,99},{4,36}... | collective-permute-start | bytes 2752520 | tf_op jit(solution)/shard_map/ppermute | solution.py:285
  104.1 2.2 copy-start.6
  104.5 31.0 %collective-permute-start.2 = (bf16[128,3584]{1,0:T(8,128)(2,1)S(1)}, bf16[128,3584]{1,0:T(8,128)(2,1)S(1)}, u32[]{:S(2)}, u32[]{:S(2)}) collective-permute-start(bf16[128,3584]{1,0:T(8,128)(2,1)S(1)} %get-tuple-element.125), channel_id=1, source_target_pairs={{32,64},{96,0},{33,65},{97,1},{34,66},{98,2},{35,67},{99,3},{36,68... | collective-permute-start | bytes 2752520 | tf_op jit(solution)/shard_map/ppermute | solution.py:285
  107.4 123.3 %collective-permute-start.1 = (bf16[128,3584]{1,0:T(8,128)(2,1)}, bf16[128,3584]{1,0:T(8,128)(2,1)}, u32[]{:S(2)}, u32[]{:S(2)}) collective-permute-start(bf16[128,3584]{1,0:T(8,128)(2,1)} %get-tuple-element.123), channel_id=1, source_target_pairs={{32,64},{96,0},{33,65},{97,1},{34,66},{98,2},{35,67},{99,3},{36,68... | collective-permute-start | bytes 2752520 | tf_op jit(solution)/shard_map/ppermute | solution.py:285
  138.8 31.3 %copy-start.14 = (bf16[1,1,3584,1024]{3,2,1,0:T(8,128)(2,1)S(1)}, bf16[1,1,3584,1024]{3,2,1,0:T(8,128)(2,1)}, u32[]{:S(2)}) copy-start(bf16[1,1,3584,1024]{3,2,1,0:T(8,128)(2,1)} %get-tuple-element.111) | copy-start | bytes 22020100 | tf_op jit(solution)/shard_map/cond
  186.8 31.0 %copy-start.5 = (s32[2,2,128]{2,1,0:T(2,128)S(1)}, s32[2,2,128]{2,1,0:T(2,128)}, u32[]{:S(2)}) copy-start(s32[2,2,128]{2,1,0:T(2,128)} %get-tuple-element.110.refs_2_.routes_ref) | copy-start | bytes 6148 | tf_op jit(solution)/shard_map/cond
  186.8 31.0 %copy-start.10 = (f32[2,2,128]{2,1,0:T(2,128)S(1)}, f32[2,2,128]{2,1,0:T(2,128)}, u32[]{:S(2)}) copy-start(f32[2,2,128]{2,1,0:T(2,128)} %get-tuple-element.115.logits_ref) | copy-start | bytes 6148 | tf_op jit(solution)/shard_map/cond
  220.7 10.0 %collective-permute-start.3 = (bf16[128,3584]{1,0:T(8,128)(2,1)S(1)}, bf16[128,3584]{1,0:T(8,128)(2,1)S(1)}, u32[]{:S(2)}, u32[]{:S(2)}) collective-permute-start(bf16[128,3584]{1,0:T(8,128)(2,1)S(1)} %get-tuple-element.126), channel_id=1, source_target_pairs={{0,32},{64,96},{1,33},{65,97},{2,34},{66,98},{3,35},{67,99},{4,36}... | collective-permute-start | bytes 2752520 | tf_op jit(solution)/shard_map/ppermute | solution.py:285
